TPU v7x, 32 devices: a whole 2x2x4 slice. The times are simulated.
32 devices in a mesh: band: 4 (over x, core), blk: 8 (over z, y).
Axes of the slice: x: 2, y: 2, z: 4, core: 2. Of those that a mesh axis runs over, the one named last changes fastest.
Arguments:
- visibility: float32 [2, 32, 8192], P(None, 'band', 'blk'), may hold values from -6 to 6
- coherency: float32 [2, 32, 100, 8192], P(None, 'band', None, 'blk'), may hold values from -0.625 to 0.625
- station_first: int32 [8192], P('blk'), may hold values from 0 to 61, as said below
- station_second: int32 [8192], P('blk'), may hold values from 0 to 61
- gains_start: float32 [2, 62, 3200], P(None, None, 'band'), may hold values from -6 to 6
- consensus_prev: float32 [2, 62, 3200], P(None, None, 'band'), may hold values from -6 to 6
- dual_prev: float32 [2, 62, 3200], P(None, None, 'band'), may hold values from -6 to 6
- penalty: float32 [100], replicated, may hold values from 0.5 to 8
- noise_var: float32 [100], replicated, may hold values from 0.05 to 1
Outputs:
- gains: float32 [2, 62, 3200], P(None, None, 'band')
- consensus: float32 [2, 62, 3200], P(None, None, 'band')
- dual: float32 [2, 62, 3200], P(None, None, 'band')
Inputs may be any that keep to these rules, and one draw needn't show every extreme that they name: station_first and station_second differ in every row.
All inputs are finite; a program needn't handle non-finite values.
Results may differ from a plain program's by a relative error of at most 0.0003.
Values sent between devices are 32-bit elements; how exact they have to be, the bound alone decides.
A program may use at most 128 MiB of HBM per device.

v0:
```python
import jax
import jax.numpy as jnp
from jax import lax
from jax.sharding import PartitionSpec as P

ITERS = 4


highest = lax.Precision.HIGHEST


def band_sums(coh, vis, gains, table_first, table_second):

    def pick(comp, table):
        return jnp.einsum("pk,pr->kr", gains[comp], table, precision=highest)

    def spread(x, table):
        return jnp.einsum("kr,pr->pk", x, table, precision=highest)

    gp_re = pick(0, table_first)
    gp_im = pick(1, table_first)
    gq_re = pick(0, table_second)
    gq_im = pick(1, table_second)
    c_re = coh[0]
    c_im = coh[1]
    t_re = c_re * gq_re + c_im * gq_im
    t_im = c_im * gq_re - c_re * gq_im
    m_re = gp_re * t_re - gp_im * t_im
    m_im = gp_re * t_im + gp_im * t_re
    e_re = vis[0] - jnp.sum(m_re, axis=0)
    e_im = vis[1] - jnp.sum(m_im, axis=0)
    r_re = e_re[None, :] + m_re
    r_im = e_im[None, :] + m_im
    u_re = c_re * gp_re - c_im * gp_im
    u_im = c_re * gp_im + c_im * gp_re
    num_re = spread(r_re * t_re + r_im * t_im, table_first) + spread(
        r_re * u_re + r_im * u_im, table_second
    )
    num_im = spread(r_im * t_re - r_re * t_im, table_first) + spread(
        r_re * u_im - r_im * u_re, table_second
    )
    den = spread(t_re * t_re + t_im * t_im, table_first) + spread(
        u_re * u_re + u_im * u_im, table_second
    )
    return jnp.stack([num_re, num_im, den])


def refresh(gains, total, target, weight):
    fresh_re = (total[0] + weight * target[0]) / (total[2] + weight)
    fresh_im = (total[1] + weight * target[1]) / (total[2] + weight)
    return 0.5 * gains + 0.5 * jnp.stack([fresh_re, fresh_im])


def smoother(noise, count):
    index = jnp.arange(count, dtype=jnp.float32)
    diff = (index[:, None] - index[None, :]) / (count / 4.0)
    kern = jnp.exp(-0.5 * diff * diff)

    def single(level):
        matrix = kern + level * jnp.eye(count, dtype=jnp.float32)
        factor = jnp.linalg.cholesky(matrix)
        return jax.scipy.linalg.cho_solve((factor, True), kern).T

    return jax.vmap(single)(noise)


def on_device(
    visibility,
    coherency,
    station_first,
    station_second,
    gains_start,
    consensus_prev,
    dual_prev,
    penalty,
    noise_var,
):
    stations = gains_start.shape[1]
    directions = penalty.shape[0]
    bands_here = visibility.shape[1]
    rows_here = visibility.shape[2]
    groups = lax.axis_size("blk")
    bands_all = bands_here * lax.axis_size("band")
    stations_iota = jnp.arange(stations, dtype=jnp.int32)
    table_first = (stations_iota[:, None] == station_first[None, :]).astype(jnp.float32)
    table_second = (stations_iota[:, None] == station_second[None, :]).astype(jnp.float32)
    rho_col = jnp.tile(penalty, bands_here)
    weight = rho_col * (rows_here * groups / (stations * directions))
    target = consensus_prev - dual_prev / rho_col
    gains = gains_start
    for step in range(ITERS):
        view = gains.reshape(2, stations, bands_here, directions)

        def one_band(index):
            coh = lax.dynamic_index_in_dim(coherency, index, 1, False)
            vis = lax.dynamic_index_in_dim(visibility, index, 1, False)
            gband = lax.dynamic_index_in_dim(view, index, 2, False)
            return band_sums(coh, vis, gband, table_first, table_second)

        parts = lax.map(one_band, jnp.arange(bands_here, dtype=jnp.int32))
        parts = parts.transpose(1, 2, 0, 3).reshape(3, stations, bands_here * directions)
        total = lax.psum(parts, "blk")
        gains = refresh(gains, total, target, weight)
    mixed = gains + dual_prev / rho_col
    smooth = smoother(noise_var, bands_all)
    offset = lax.axis_index("band") * bands_here
    cols_sel = lax.dynamic_slice_in_dim(smooth, offset, bands_here, 2)
    local_view = mixed.reshape(2, stations, bands_here, directions)
    term = jnp.einsum("kfg,cpgk->cpfk", cols_sel, local_view, precision=highest)
    term = term.reshape(2, stations, bands_all * directions)
    consensus = lax.psum_scatter(term, "band", scatter_dimension=2, tiled=True)
    dual = dual_prev + rho_col * (gains - consensus)
    return (gains, consensus, dual)


def solution(mesh):
    return jax.shard_map(
        on_device,
        mesh=mesh,
        in_specs=(
            P(None, "band", "blk"),
            P(None, "band", None, "blk"),
            P("blk"),
            P("blk"),
            P(None, None, "band"),
            P(None, None, "band"),
            P(None, None, "band"),
            P(),
            P(),
        ),
        out_specs=(P(None, None, "band"), P(None, None, "band"), P(None, None, "band")),
        check_vma=False,
    )
```

profile of v0, /device:TPU:0, one launch (start us, length us, event | category | flops | bytes accessed | tf_op | source)
XLA Modules:
  0.0 955.4 jit_solution(10018881492889720721)
XLA Ops:
  7.2 9.5 copy.70
  17.6 79.9 %while.44 = (s32[]{:T(128)}, f32[8,3,62,100]{3,2,1,0:T(8,128)S(1)}, s32[8]{0:T(128)S(1)}, f32[2,8,1024]{2,1,0:T(8,128)S(1)}, f32[2,62,8,100]{3,2,0,1:T(8,128)S(1...) while((s32[]{:T(128)}, f32[8,3,62,100]{3,2,1,0:T(8,128)S(1)}, ...), condition=%wide.region_3.4_spmd.clone, body=%wide.region_0.3_spmd.clone.sunk | while | flops 767891968 | bytes 16715691 | solution.py:100
  21.9 1.9 multiply_subtract_fusion.24
  31.9 1.9 multiply_subtract_fusion.24
  41.9 1.9 multiply_subtract_fusion.24
  51.9 1.9 multiply_subtract_fusion.24
  61.8 1.9 multiply_subtract_fusion.24
  71.8 1.9 multiply_subtract_fusion.24
  81.8 1.9 multiply_subtract_fusion.24
  91.8 1.9 multiply_subtract_fusion.24
  99.7 76.1 %all-reduce.5.cloned.1.call-done = f32[3,62,800]{2,1,0:T(8,128)} async-done(((f32[3,62,800]{2,1,0:T(8,128)}), f32[3,62,800]{2,1,0:T(8,128)}) %all-reduce.5.cloned.1.call-update) | async-done | bytes 595216 | tf_op jit(solution)/shard_map/psum | solution.py:102
  177.5 79.8 %while.45 = (s32[]{:T(128)}, f32[8,3,62,100]{3,2,1,0:T(8,128)S(1)}, s32[8]{0:T(128)S(1)}, f32[2,8,1024]{2,1,0:T(8,128)S(1)}, f32[2,62,8,100]{3,2,1,0:T(8,128)S(1...) while((s32[]{:T(128)}, f32[8,3,62,100]{3,2,1,0:T(8,128)S(1)}, ...), condition=%wide.region_8.9_spmd.clone, body=%wide.region_5.8_spmd.clone.sunk | while | flops 767891968 | bytes 16715691 | solution.py:100
  181.8 1.9 multiply_subtract_fusion.25
  191.8 1.9 multiply_subtract_fusion.25
  201.8 1.9 multiply_subtract_fusion.25
  211.7 1.9 multiply_subtract_fusion.25
  221.7 1.9 multiply_subtract_fusion.25
  231.7 1.9 multiply_subtract_fusion.25
  241.7 1.9 multiply_subtract_fusion.25
  251.7 1.9 multiply_subtract_fusion.25
  259.8 293.8 %custom-call.11 = f32[100,32,32]{2,1,0:T(8,128)} custom-call(f32[100,32,32]{2,1,0:T(8,128)S(1)} %add_multiply_fusion), custom_call_target="Cholesky" | custom-call | tf_op jit(solution)/shard_map/vmap(jit(cholesky))/cholesky | solution.py:61
  553.6 2.3 copy.81
  559.4 93.0 %while.46 = (s32[]{:T(128)}, f32[8,3,62,100]{3,2,1,0:T(8,128)}, s32[8]{0:T(128)S(1)}, f32[2,8,1024]{2,1,0:T(8,128)S(1)}, f32[2,62,8,100]{3,2,1,0:T(8,128)}, /*in...) while((s32[]{:T(128)}, f32[8,3,62,100]{3,2,1,0:T(8,128)}, ...), condition=%wide.region_13.14_spmd.clone, body=%wide.region_10.13_spmd.clone.sunk | while | flops 767891968 | bytes 16692295 | solution.py:100
  564.7 1.9 multiply_subtract_fusion.26
  576.3 1.9 multiply_subtract_fusion.26
  587.9 1.9 multiply_subtract_fusion.26
  599.6 1.9 multiply_subtract_fusion.26
  611.2 1.9 multiply_subtract_fusion.26
  622.8 1.9 multiply_subtract_fusion.26
  634.4 1.9 multiply_subtract_fusion.26
  646.0 1.9 multiply_subtract_fusion.26
  656.2 13.3 %custom-call.12 = f32[100,1,32,32]{0,2,3,1:T(8,128)} custom-call(f32[100,1,32,32]{0,3,2,1:T(8,128)S(1)} %select_bitcast_fusion), custom_call_target="InvertDiagBlocksLowerTriangular" | custom-call | tf_op jit(solution)/shard_map/vmap(jit(_cho_solve))/triangular_solve | solution.py:62
  669.5 2.4 copy.84
  671.8 56.2 %all-reduce.9.cloned.1.call-done = f32[3,62,800]{2,1,0:T(8,128)} async-done(((f32[3,62,800]{2,1,0:T(8,128)}), f32[3,62,800]{2,1,0:T(8,128)}) %all-reduce.9.cloned.1.call-update) | async-done | bytes 595216 | tf_op jit(solution)/shard_map/psum | solution.py:102
  731.0 2.1 reshape.290
  734.1 91.2 %while.47 = (s32[]{:T(128)}, f32[8,3,62,100]{3,2,1,0:T(8,128)}, s32[8]{0:T(128)S(1)}, f32[2,8,1024]{2,1,0:T(8,128)S(1)}, f32[2,62,8,100]{3,2,1,0:T(8,128)}, /*in...) while((s32[]{:T(128)}, f32[8,3,62,100]{3,2,1,0:T(8,128)}, ...), condition=%wide.region_18.19_spmd.clone, body=%wide.region_15.18_spmd.clone.sunk | while | flops 767891968 | bytes 16692295 | solution.py:100
  784.8 1.9 multiply_subtract_fusion.27
  796.2 1.9 multiply_subtract_fusion.27
  807.6 1.9 multiply_subtract_fusion.27
  825.3 2.5 copy.80
  827.8 2.3 reshape.291
  830.3 2.7 fusion.308
  833.0 2.8 fusion.335
  835.9 67.1 %all-reduce.11.cloned.1.call-done = f32[3,62,800]{2,1,0:T(8,128)} async-done(((f32[3,62,800]{2,1,0:T(8,128)}), f32[3,62,800]{2,1,0:T(8,128)}) %all-reduce.11.cloned.1.call-update) | async-done | bytes 595216 | tf_op jit(solution)/shard_map/psum | solution.py:102
  906.0 3.8 convolution_bitcast_fusion
  909.9 2.5 copy.95
  912.4 3.0 reshape.296
  917.6 25.6 %reduce-scatter.4.cloned.1.call-done = f32[800,124]{1,0:T(8,128)} async-done(((f32[3200,124]{1,0:T(8,128)}), f32[800,124]{1,0:T(8,128)}) %reduce-scatter.4.cloned.1.call-update) | async-done | bytes 396816
  (613 shorter events, 258.4 us)
Async XLA Ops:
  7.2 9.6 %copy-start.2 = (f32[2,62,800]{2,0,1:T(2,128)S(1)}, f32[2,62,800]{2,0,1:T(2,128)}, u32[]{:S(2)}) copy-start(f32[2,62,800]{2,0,1:T(2,128)} %param.21) | copy-start | bytes 1190404
  7.2 168.7 %all-reduce.5.cloned.1.call-start = ((), (), s32[]{:S(2)}) async-start(), calls=%async_computation.1 | async-start | bytes 1376256 | tf_op jit(solution)/shard_map/psum | solution.py:102
  16.8 0.7 copy-start
  16.8 0.7 copy-start.1
  16.8 0.9 copy-start.17
  97.5 2.0 copy-start.19
  97.5 2.1 copy-start.4
  97.6 2.1 copy-start.16
  99.3 456.7 %all-reduce.7.cloned.1.call-start = ((), (), s32[]{:S(2)}) async-start(), calls=%async_computation.2 | async-start | bytes 1376256 | tf_op jit(solution)/shard_map/psum | solution.py:102
  257.4 2.0 copy-start.18
  259.0 469.0 %all-reduce.9.cloned.1.call-start = ((), (), s32[]{:S(2)}) async-start(), calls=%async_computation.3 | async-start | bytes 1376256 | tf_op jit(solution)/shard_map/psum | solution.py:102
  557.2 2.2 copy-start.6
  557.2 2.2 copy-start.9
  655.2 247.7 %all-reduce.11.cloned.1.call-start = ((), (), s32[]{:S(2)}) async-start(), calls=%async_computation.4 | async-start | bytes 1376256 | tf_op jit(solution)/shard_map/psum | solution.py:102
  728.1 2.1 copy-start.7
  728.1 2.1 copy-start.10
  729.4 0.7 copy-start.12
  729.4 0.8 copy-start.14
  830.1 113.1 %reduce-scatter.4.cloned.1.call-start = ((), (), s32[]{:S(2)}) async-start(), calls=%async_computation.5 | async-start | bytes 2048000
  835.9 68.3 %copy-start.8 = (f32[1,62,800]{2,1,0:T(8,128)S(1)}, f32[1,62,800]{2,1,0:T(8,128)}, u32[]{:S(2)}) copy-start(f32[1,62,800]{2,1,0:T(8,128)} %copy-done.6) | copy-start | bytes 595204
  835.9 68.3 %copy-start.11 = (f32[1,62,800]{2,1,0:T(8,128)S(1)}, f32[1,62,800]{2,1,0:T(8,128)}, u32[]{:S(2)}) copy-start(f32[1,62,800]{2,1,0:T(8,128)} %copy-done.9) | copy-start | bytes 595204
  835.9 68.3 %copy-start.13 = (f32[1,62,800]{2,1,0:T(8,128)S(1)}, f32[1,62,800]{2,1,0:T(8,128)}, u32[]{:S(2)}) copy-start(f32[1,62,800]{2,1,0:T(8,128)} %copy-done.12) | copy-start | bytes 595204
  835.9 68.3 %copy-start.15 = (f32[1,62,800]{2,1,0:T(8,128)S(1)}, f32[1,62,800]{2,1,0:T(8,128)}, u32[]{:S(2)}) copy-start(f32[1,62,800]{2,1,0:T(8,128)} %copy-done.14) | copy-start | bytes 595204
  915.5 1.0 copy-start.3
  917.6 29.8 %copy-start.5 = (f32[2,62,800]{2,0,1:T(2,128)S(1)}, f32[2,62,800]{2,0,1:T(2,128)}, u32[]{:S(2)}) copy-start(f32[2,62,800]{2,0,1:T(2,128)} %param.23) | copy-start | bytes 1190404
Sparse Core Ops, SparseCore 0:
  99.4 76.3 all-reduce.4
  259.2 73.7 all-reduce.6
  655.3 72.6 all-reduce.8
  830.2 72.6 all-reduce.10
  915.6 27.5 reduce-scatter.3
where the time goes:
time: 965 us; the launch traced here: 955 us
  other arithmetic  331 us (34%)
  matrix products  237 us (25%)
  waiting for transfers between devices  225 us (23%)
  local copies, waits for them, and re-layouts  84.1 us (9%)
  loops' own time  63.1 us (7%)
  between operations  14.4 us (1%)
    another operation x4, other arithmetic, single(): factor = jnp.linalg.cholesky(matrix)  294 us
    psum x4, waiting for transfers between devices, on_device(): total = lax.psum(parts, 'blk')  199 us
    dot_general x192, matrix products, spread(): return jnp.einsum('kr,pr->pk', x, table, precision=highest)  114 us
    dot_general x128, matrix products, pick(): return jnp.einsum('pk,pr->kr', gains[comp], table, precision=highest)  113 us
    another operation x4, loops' own time, on_device(): parts = lax.map(one_band, jnp.arange(bands_here, dtype=jnp.int32))  63.1 us
    unnamed x6, waiting for transfers between devices  25.7 us
    unnamed x48, local copies, waits for them, and re-layouts  23.5 us
  transfers between devices with their start and end apart: 5, of which 4 were waited for; matrix products, arithmetic and copies ran while one was open for 33% of the time, Pallas kernels for 0%

commit v1 on v0

v1 whole, which is shorter than its diff:
```python
import functools
import jax
import jax.numpy as jnp
from jax import lax
from jax.experimental import pallas as pl
from jax.experimental.pallas import tpu as pltpu
from jax.sharding import PartitionSpec as P

ITERS = 4
LANES = 128
HALF = 64
CHUNK = 256
TILE = 16


def round_up(x, m):
    return (x + m - 1) // m * m


def smoother_kernel(count, noise_ref, out_ref, work):
    level = noise_ref[...]
    cols = lax.broadcasted_iota(jnp.int32, (count, LANES), 0)
    for i in range(count):
        diff = (cols - i).astype(jnp.float32) / (count / 4.0)
        kern = jnp.exp(-0.5 * diff * diff)
        work[i, :count, :] = kern + jnp.where(cols == i, level, 0.0)
        work[i, count:, :] = kern

    def eliminate(p, carry):
        pivot = work[p, pl.ds(p, 1), :]
        row = work[p] / pivot
        for i in range(count):
            work[i] = work[i] - work[i, pl.ds(p, 1), :] * row
        work[p] = row
        return carry

    lax.fori_loop(0, count, eliminate, 0)
    for i in range(count):
        out_ref[i] = work[i, count:, :]


def smoother(noise, count):
    pad = jnp.pad(noise, (0, LANES * ((noise.shape[0] + LANES - 1) // LANES) - noise.shape[0]), constant_values=1.0)
    groups = pad.shape[0] // LANES
    return pl.pallas_call(
        functools.partial(smoother_kernel, count),
        out_shape=jax.ShapeDtypeStruct((count, count, groups * LANES), jnp.float32),
        grid=(groups,),
        in_specs=[pl.BlockSpec((1, LANES), lambda g: (0, g))],
        out_specs=pl.BlockSpec((count, count, LANES), lambda g: (0, 0, g)),
        scratch_shapes=[pltpu.VMEM((count, 2 * count, LANES), jnp.float32)],
        compiler_params=pltpu.CompilerParams(vmem_limit_bytes=16 << 20),
        name="smoother",
    )(pad[None, :])


def band_sums(g_re, g_im, load_c, load_v, rows, t1, t2, tt, gp, gq, xs):
    half_k = g_re.shape[0]
    full_k = 2 * half_k
    lane = lax.broadcasted_iota(jnp.int32, (half_k, LANES), 1)
    low = lane < HALF
    parts = []
    for g in (g_re, g_im):
        r = pltpu.roll(g, HALF, 1)
        for full in (jnp.where(low, g, r), jnp.where(low, r, g)):
            hi = full.astype(jnp.bfloat16).astype(jnp.float32)
            parts.append(jnp.where(low, hi, full - hi))
    lhs = jnp.concatenate(parts, axis=0).astype(jnp.bfloat16)
    total = None
    for rc in range(rows // CHUNK):
        buf = rc % 2
        rsl = pl.ds(rc * CHUNK, CHUNK)
        gp[buf] = jnp.dot(lhs, t1[:, rsl], preferred_element_type=jnp.float32)
        gq[buf] = jnp.dot(lhs, t2[:, rsl], preferred_element_type=jnp.float32)
        sum_re = jnp.zeros((TILE, CHUNK), jnp.float32)
        sum_im = jnp.zeros((TILE, CHUNK), jnp.float32)

        def put(kind, kt, side, x):
            hi = x.astype(jnp.bfloat16)
            lo = (x - hi.astype(jnp.float32)).astype(jnp.bfloat16)
            rsel = pl.ds(kind * full_k + kt * TILE, TILE)
            xs[buf, rsel, pl.ds(2 * side * CHUNK, CHUNK)] = hi
            xs[buf, rsel, pl.ds((2 * side + 1) * CHUNK, CHUNK)] = lo

        for kt in range(full_k // TILE):
            c_re, c_im = load_c(kt, rsl)
            sl_re, sl_im = pl.ds(kt * TILE, TILE), pl.ds(full_k + kt * TILE, TILE)
            p_re, p_im, q_re, q_im = gp[buf, sl_re], gp[buf, sl_im], gq[buf, sl_re], gq[buf, sl_im]
            t_re = c_re * q_re + c_im * q_im
            t_im = c_im * q_re - c_re * q_im
            sum_re += p_re * t_re - p_im * t_im
            sum_im += p_re * t_im + p_im * t_re
            put(2, kt, 0, t_re * t_re + t_im * t_im)
            put(2, kt, 1, (c_re * c_re + c_im * c_im) * (p_re * p_re + p_im * p_im))
        v_re, v_im = load_v(rsl)
        e_re = v_re - jnp.sum(sum_re, axis=0, keepdims=True)
        e_im = v_im - jnp.sum(sum_im, axis=0, keepdims=True)
        for kt in range(full_k // TILE):
            c_re, c_im = load_c(kt, rsl)
            sl_re, sl_im = pl.ds(kt * TILE, TILE), pl.ds(full_k + kt * TILE, TILE)
            p_re, p_im, q_re, q_im = gp[buf, sl_re], gp[buf, sl_im], gq[buf, sl_re], gq[buf, sl_im]
            d_re = e_re * c_re + e_im * c_im
            d_im = e_im * c_re - e_re * c_im
            put(0, kt, 0, d_re * q_re - d_im * q_im)
            put(1, kt, 0, d_re * q_im + d_im * q_re)
            put(0, kt, 1, d_re * p_re + d_im * p_im)
            put(1, kt, 1, d_re * p_im - d_im * p_re)
        part = jnp.dot(xs[buf], tt[rc], preferred_element_type=jnp.float32)
        total = part if total is None else total + part

    def pack(kind):
        x = total[kind * full_k : (kind + 1) * full_k]
        return jnp.where(low, x[:half_k], x[half_k:])

    den = pack(2)
    return pack(0) + g_re * den, pack(1) + g_im * den, den


def sums_kernel(whole_tiles, g_ref, coh_ref, tail_ref, vis_ref, t1, t2, tt, out_ref, gp, gq, xs):
    rows = t1.shape[1]

    def load_c(kt, rsl):
        if kt < whole_tiles:
            return (coh_ref[0, 0, pl.ds(kt * TILE, TILE), rsl], coh_ref[1, 0, pl.ds(kt * TILE, TILE), rsl])
        sl = pl.ds((kt - whole_tiles) * TILE, TILE)
        return tail_ref[0, 0, sl, rsl], tail_ref[1, 0, sl, rsl]

    def load_v(rsl):
        return vis_ref[0, 0, :, rsl], vis_ref[1, 0, :, rsl]

    half_k = out_ref.shape[2]
    re, im, den = band_sums(g_ref[0, 0], g_ref[0, 1], load_c, load_v, rows, t1, t2, tt, gp, gq, xs)
    out_ref[0, 0] = re
    out_ref[0, 1] = im
    out_ref[0, 2] = den


def tables(station_first, station_second):
    def gather_table(station):
        return (lax.broadcasted_iota(jnp.int32, (LANES, 1), 0) % HALF == station[None, :]).astype(jnp.bfloat16)

    first = station_first.reshape(-1, 1, CHUNK)
    second = station_second.reshape(-1, 1, CHUNK)
    both = jnp.concatenate([first, first, second, second], axis=1).reshape(first.shape[0], 4 * CHUNK, 1)
    spread = (both == lax.broadcasted_iota(jnp.int32, (1, 1, LANES), 2) % HALF).astype(jnp.bfloat16)
    return gather_table(station_first), gather_table(station_second), spread


def packer(stations, bands, directions, half_k):
    def pack(x, fill=0.0):
        c = x.shape[0]
        x = x.reshape(c, x.shape[1], bands, directions)
        x = jnp.pad(x, ((0, 0), (0, HALF - x.shape[1]), (0, 0), (0, 2 * half_k - directions)), constant_values=fill)
        x = x.reshape(c, HALF, bands, 2, half_k).transpose(2, 0, 4, 3, 1)
        return x.reshape(bands, c, half_k, LANES)

    def unpack(x):
        c = x.shape[1]
        x = x.reshape(bands, c, half_k, 2, HALF).transpose(1, 4, 0, 3, 2)
        x = x.reshape(c, HALF, bands, 2 * half_k)[:, :stations, :, :directions]
        return x.reshape(c, stations, bands * directions)

    return pack, unpack


def on_device(visibility, coherency, station_first, station_second, gains_start, consensus_prev, dual_prev, penalty, noise_var):
    stations = gains_start.shape[1]
    directions = penalty.shape[0]
    bands = visibility.shape[1]
    rows = visibility.shape[2]
    groups = lax.axis_size("blk")
    bands_all = bands * lax.axis_size("band")
    full_k = round_up(directions, TILE)
    half_k = full_k // 2
    whole_tiles = directions // TILE
    t1, t2, tt = tables(station_first, station_second)
    tail = jnp.pad(coherency[:, :, whole_tiles * TILE :, :], ((0, 0), (0, 0), (0, full_k - directions), (0, 0)))
    tail = tail if full_k > whole_tiles * TILE else coherency[:, :, :TILE, :]
    pack, unpack = packer(stations, bands, directions, half_k)
    rho_col = jnp.tile(penalty, bands)
    scaled = dual_prev / rho_col
    target = pack(consensus_prev - scaled)
    rho_pack = jnp.pad(penalty, (0, full_k - directions), constant_values=1.0).reshape(2, half_k).T
    weight = jnp.repeat(rho_pack * (rows * groups / (stations * directions)), HALF, axis=1)
    gains = pack(gains_start)
    vis = visibility[:, :, None, :]
    whole = lambda f: (0, 0)
    call = pl.pallas_call(
        functools.partial(sums_kernel, whole_tiles),
        out_shape=jax.ShapeDtypeStruct((bands, 3, half_k, LANES), jnp.float32),
        grid=(bands,),
        in_specs=[
            pl.BlockSpec((1, 2, half_k, LANES), lambda f: (f, 0, 0, 0)),
            pl.BlockSpec((2, 1, directions, rows), lambda f: (0, f, 0, 0)),
            pl.BlockSpec((2, 1, tail.shape[2], rows), lambda f: (0, f, 0, 0)),
            pl.BlockSpec((2, 1, 1, rows), lambda f: (0, f, 0, 0)),
            pl.BlockSpec((LANES, rows), whole),
            pl.BlockSpec((LANES, rows), whole),
            pl.BlockSpec((rows // CHUNK, 4 * CHUNK, LANES), lambda f: (0, 0, 0)),
        ],
        out_specs=pl.BlockSpec((1, 3, half_k, LANES), lambda f: (f, 0, 0, 0)),
        scratch_shapes=[
            pltpu.VMEM((2, 2 * full_k, CHUNK), jnp.float32),
            pltpu.VMEM((2, 2 * full_k, CHUNK), jnp.float32),
            pltpu.VMEM((2, 3 * full_k, 4 * CHUNK), jnp.bfloat16),
        ],
        compiler_params=pltpu.CompilerParams(vmem_limit_bytes=48 << 20),
        name="band_sums",
    )
    for step in range(ITERS):
        parts = call(gains, coherency, tail, vis, t1, t2, tt)
        total = lax.psum(parts, "blk")
        fresh = (total[:, :2] + weight * target) / (total[:, 2:] + weight)
        gains = 0.5 * gains + 0.5 * fresh
    gains = unpack(gains)
    mixed = gains + scaled
    smooth = smoother(noise_var, bands_all)[:, :, :directions]
    offset = lax.axis_index("band") * bands
    cols = lax.dynamic_slice_in_dim(smooth, offset, bands, 0)
    local_view = mixed.reshape(2, stations, bands, directions)
    term = jnp.einsum("gfk,cpgk->cpfk", cols, local_view, precision=lax.Precision.HIGHEST)
    term = term.reshape(2, stations, bands_all * directions)
    consensus = lax.psum_scatter(term, "band", scatter_dimension=2, tiled=True)
    dual = dual_prev + rho_col * (gains - consensus)
    return (gains, consensus, dual)


def solution(mesh):
    return jax.shard_map(
        on_device,
        mesh=mesh,
        in_specs=(
            P(None, "band", "blk"),
            P(None, "band", None, "blk"),
            P("blk"),
            P("blk"),
            P(None, None, "band"),
            P(None, None, "band"),
            P(None, None, "band"),
            P(),
            P(),
        ),
        out_specs=(P(None, None, "band"), P(None, None, "band"), P(None, None, "band")),
        check_vma=False,
    )
```

time: 965 us -> 471 us (0.49)
  other arithmetic: 331 us -> 12.5 us
  matrix products: 237 us -> 2.81 us
  Pallas kernels: 0 us -> 83.3 us
  waiting for transfers between devices: 225 us -> 300 us
  loops' own time: 63.1 us -> 0 us
  local copies, waits for them, and re-layouts: 84.1 us -> 56.7 us
    another operation x7 -> x0, other arithmetic: 307 us -> none  [the longest x4 294 us: single(): factor = jnp.linalg.cholesky(matrix)]
    dot_general x321 -> x1, matrix products: 231 us -> 2.81 us  [on_device(): jnp.einsum('gfk,cpgk->cpfk', cols, local_view, precision=lax.Precision.HI...]
    pallas_call x0 -> x5, Pallas kernels: none -> 83.3 us  [the longest x4 77.9 us: on_device(): parts = call(gains, coherency, tail, vis, t1, t2, tt)]
    psum x4, waiting for transfers between devices: 199 us -> 273 us  [on_device(): total = lax.psum(parts, 'blk')]
    another operation x4 -> x0, loops' own time: 63.1 us -> none  [on_device(): parts = lax.map(one_band, jnp.arange(bands_here, dtype=jnp.int32))]
    slice x56 -> x2, local copies, waits for them, and re-layouts: 18.8 us -> 0.07 us  [the longest x1 0.04 us: on_device(): coherency[:, :, whole_tiles * TILE:, :]]
    dynamic_slice x32 -> x2, local copies, waits for them, and re-layouts: 18.8 us -> 0.97 us  [on_device(): cols = lax.dynamic_slice_in_dim(smooth, offset, bands, 0)]
    dynamic_update_slice x32 -> x0, other arithmetic: 10.6 us -> none  [on_device(): parts = lax.map(one_band, jnp.arange(bands_here, dtype=jnp.int32))]
  transfers between devices with their start and end apart: 5 -> 5, of which waited for: 4 -> 5; matrix products, arithmetic and copies ran while one was open for 33% -> 4% of each run, Pallas kernels for 0% -> 1%
where the time goes in v1:
time: 471 us; the launch traced here: 470 us
  waiting for transfers between devices  300 us (64%)
  Pallas kernels  83.3 us (18%)
  local copies, waits for them, and re-layouts  56.7 us (12%)
  between operations  14.3 us (3%)
  other arithmetic  12.5 us (3%)
    psum x4, waiting for transfers between devices, on_device(): total = lax.psum(parts, 'blk')  273 us
    pallas_call x4, Pallas kernels, on_device(): parts = call(gains, coherency, tail, vis, t1, t2, tt)  77.9 us
    unnamed x49, local copies, waits for them, and re-layouts  30 us
    unnamed x6, waiting for transfers between devices  26.7 us
  transfers between devices with their start and end apart: 5, of which 5 were waited for; matrix products, arithmetic and copies ran while one was open for 4% of the time, Pallas kernels for 1%

profile of v1, /device:TPU:0, one launch (start us, length us, event | category | flops | bytes accessed | tf_op | source)
XLA Modules:
  0.0 470.1 jit_solution(4123964702621359583)
XLA Ops:
  7.3 6.7 %copy.61.coh_ref = f32[2,8,100,1024]{3,2,1,0:T(8,128)S(1)} copy(f32[2,8,100,1024]{3,1,2,0:T(8,128)} %param.10) | data formatting | bytes 13107200 | tf_op args[1]
  14.3 2.6 copy-done.7
  16.8 0.8 compare_convert_fusion.tt
  18.4 0.9 pad.19
  19.3 2.6 reshape.89
  21.9 3.1 copy.59
  25.0 1.7 reshape.90.g_ref
  26.8 19.5 %band_sums.4 = f32[8,3,56,128]{3,2,1,0:T(8,128)S(1)} custom-call(f32[8,2,56,128]{3,2,1,0:T(8,128)S(1)} %reshape.90.g_ref, f32[2,8,100,1024]{3,2,1,0:T(8,128)} %copy-done.7, f32[2,8,16,1024]{3,2,1,0:T(8,128)S(1)} %pad.20.tail_ref, f32[2,8,1,1024]{3,2,1,0:T(1,128)S(1)} %broadcast_in_dim.11.vis_ref, bf16[128,1024]{1,0:T(8,128)(2,1)S(1)} %get-tuple-element.13.t1, ...), custom_call_target="tpu_custom_call" | custom-call | tf_op jit(solution)/shard_map/band_sums/pallas_call | solution.py:211
  46.2 0.8 copy-done.1
  47.8 2.0 copy_subtract_fusion
  49.8 2.1 reshape.93
  51.9 1.9 pad.22
  53.8 2.6 reshape.94
  56.5 3.1 copy.65
  59.6 2.5 reshape.95
  62.1 61.6 %all-reduce.10.cloned.1.call-done = f32[8,3,56,128]{3,2,1,0:T(8,128)} async-done(((f32[8,3,56,128]{3,2,1,0:T(8,128)}), f32[8,3,56,128]{3,2,1,0:T(8,128)}) %all-reduce.10.cloned.1.call-update) | async-done | bytes 688144 | tf_op jit(solution)/shard_map/psum | solution.py:212
  123.7 1.0 fusion.13
  124.6 0.7 copy-done.12
  125.3 1.2 broadcast_multiply_fusion.1.g_ref
  126.6 19.5 %band_sums.5 = f32[8,3,56,128]{3,2,1,0:T(8,128)S(1)} custom-call(f32[8,2,56,128]{3,2,1,0:T(8,128)S(1)} %broadcast_multiply_fusion.1.g_ref, f32[2,8,100,1024]{3,2,1,0:T(8,128)} %copy-done.7, f32[2,8,16,1024]{3,2,1,0:T(8,128)S(1)} %pad.20.tail_ref, f32[2,8,1,1024]{3,2,1,0:T(1,128)S(1)} %broadcast_in_dim.11.vis_ref, ...), custom_call_target="tpu_custom_call" | custom-call | tf_op jit(solution)/shard_map/band_sums/pallas_call | solution.py:211
  146.1 0.9 copy-done.2
  147.0 72.8 %all-reduce.12.cloned.1.call-done = f32[8,3,56,128]{3,2,1,0:T(8,128)} async-done(((f32[8,3,56,128]{3,2,1,0:T(8,128)}), f32[8,3,56,128]{3,2,1,0:T(8,128)}) %all-reduce.12.cloned.1.call-update) | async-done | bytes 688144 | tf_op jit(solution)/shard_map/psum | solution.py:212
  219.8 1.0 fusion.12
  220.8 1.5 fusion.7.g_ref
  222.4 19.5 %band_sums.6 = f32[8,3,56,128]{3,2,1,0:T(8,128)S(1)} custom-call(f32[8,2,56,128]{3,2,1,0:T(8,128)S(1)} %fusion.7.g_ref, f32[2,8,100,1024]{3,2,1,0:T(8,128)} %copy-done.7, f32[2,8,16,1024]{3,2,1,0:T(8,128)S(1)} %pad.20.tail_ref, f32[2,8,1,1024]{3,2,1,0:T(1,128)S(1)} %copy-done.5, bf16[128,1024]{1,0:T(8,128)(2,1)S(1)} %get-tuple-element.13.t1, ...), custom_call_target="tpu_custom_call" | custom-call | tf_op jit(solution)/shard_map/band_sums/pallas_call | solution.py:211
  241.8 0.9 copy-done.3
  242.8 72.8 %all-reduce.14.cloned.1.call-done = f32[8,3,56,128]{3,2,1,0:T(8,128)} async-done(((f32[8,3,56,128]{3,2,1,0:T(8,128)}), f32[8,3,56,128]{3,2,1,0:T(8,128)}) %all-reduce.14.cloned.1.call-update) | async-done | bytes 688144 | tf_op jit(solution)/shard_map/psum | solution.py:212
  315.6 1.0 fusion.11
  316.5 0.7 copy-done.11
  317.2 1.3 broadcast_multiply_fusion.g_ref
  318.5 0.8 copy-done.6
  319.3 19.5 %band_sums.7 = f32[8,3,56,128]{3,2,1,0:T(8,128)S(1)} custom-call(f32[8,2,56,128]{3,2,1,0:T(8,128)S(1)} %broadcast_multiply_fusion.g_ref, f32[2,8,100,1024]{3,2,1,0:T(8,128)} %copy-done.7, f32[2,8,16,1024]{3,2,1,0:T(8,128)S(1)} %pad.20.tail_ref, f32[2,8,1,1024]{3,2,1,0:T(1,128)S(1)} %copy-done.6, bf16[128,1024]{1,0:T(8,128)(2,1)S(1)} %get-tuple-element.13.t1, ...), custom_call_target="tpu_custom_call" | custom-call | tf_op jit(solution)/shard_map/band_sums/pallas_call | solution.py:211
  338.8 0.9 copy-done
  340.0 5.4 %smoother.1 = f32[32,32,128]{2,1,0:T(8,128)S(1)} custom-call(f32[1,128]{1,0:T(1,128)S(1)} %pad_bitcast_fusion.noise_ref), custom_call_target="tpu_custom_call" | custom-call | tf_op jit(solution)/shard_map/smoother/pallas_call | solution.py:45
  345.5 1.0 copy.77
  346.4 66.0 %all-reduce.16.cloned.1.call-done = f32[8,3,56,128]{3,2,1,0:T(8,128)} async-done(((f32[8,3,56,128]{3,2,1,0:T(8,128)}), f32[8,3,56,128]{3,2,1,0:T(8,128)}) %all-reduce.16.cloned.1.call-update) | async-done | bytes 688144 | tf_op jit(solution)/shard_map/psum | solution.py:212
  412.5 1.0 fusion.10
  413.4 1.5 fusion.2
  415.5 1.7 copy.69
  419.0 2.8 convolution_bitcast_fusion
  421.8 4.2 copy.82
  426.0 4.4 reshape.102
  430.4 1.1 copy.74
  431.5 26.6 %reduce-scatter.4.cloned.1.call-done = f32[800,124]{1,0:T(8,128)} async-done(((f32[3200,124]{1,0:T(8,128)}), f32[800,124]{1,0:T(8,128)}) %reduce-scatter.4.cloned.1.call-update) | async-done | bytes 396816
  458.2 1.5 reshape.103
  459.7 1.0 copy.81
  460.7 1.6 copy.75
  462.4 1.1 copy.76
  (68 shorter events, 4.5 us)
Async XLA Ops:
  7.2 116.5 %all-reduce.10.cloned.1.call-start = ((), (), s32[]{:S(2)}) async-start(), calls=%async_computation.1 | async-start | bytes 1376256 | tf_op jit(solution)/shard_map/psum | solution.py:212
  7.2 6.8 %copy-start.16 = (s32[1024]{0:T(1024)S(1)}, s32[1024]{0:T(1024)}, u32[]{:S(2)}) copy-start(s32[1024]{0:T(1024)} %param.12) | copy-start | bytes 12292
  7.2 6.8 %copy-start.17 = (s32[1024]{0:T(1024)S(1)}, s32[1024]{0:T(1024)}, u32[]{:S(2)}) copy-start(s32[1024]{0:T(1024)} %param.11) | copy-start | bytes 12292
  7.2 10.4 %copy-start.15 = (f32[2,8,1024]{2,1,0:T(8,128)S(1)}, f32[2,8,1024]{2,1,0:T(8,128)}, u32[]{:S(2)}) copy-start(f32[2,8,1024]{2,1,0:T(8,128)} %param.9) | copy-start | bytes 196612
  7.3 10.4 %copy-start.14 = (f32[2,62,800]{2,0,1:T(2,128)S(1)}, f32[2,62,800]{2,0,1:T(2,128)}, u32[]{:S(2)}) copy-start(f32[2,62,800]{2,0,1:T(2,128)} %param.13) | copy-start | bytes 1190404
  14.0 2.8 copy-start.7
  17.7 108.9 %copy-start.4 = (f32[2,8,1,1024]{3,2,1,0:T(1,128)}, f32[2,8,1,1024]{3,2,1,0:T(1,128)S(1)}, u32[]{:S(2)}) copy-start(f32[2,8,1,1024]{3,2,1,0:T(1,128)S(1)} %broadcast_in_dim.11.vis_ref) | copy-start | bytes 196612
  26.7 20.6 %copy-start.18 = (f32[100]{0:T(128)S(1)}, f32[100]{0:T(128)}, u32[]{:S(2)}) copy-start(f32[100]{0:T(128)} %param.16) | copy-start | bytes 1204
  46.2 0.8 copy-start.1
  47.1 172.7 %all-reduce.12.cloned.1.call-start = ((), (), s32[]{:S(2)}) async-start(), calls=%async_computation.2 | async-start | bytes 1376256 | tf_op jit(solution)/shard_map/psum | solution.py:212
  47.7 172.1 %copy-start.9 = (f32[56,128]{1,0:T(8,128)}, f32[56,128]{1,0:T(8,128)S(1)}, u32[]{:S(2)}) copy-start(f32[56,128]{1,0:T(8,128)S(1)} %mul.69) | copy-start | bytes 86020
  124.6 0.7 copy-start.12
  146.0 0.9 copy-start.2
  147.0 168.6 %all-reduce.14.cloned.1.call-start = ((), (), s32[]{:S(2)}) async-start(), calls=%async_computation.3 | async-start | bytes 1376256 | tf_op jit(solution)/shard_map/psum | solution.py:212
  219.8 2.5 copy-start.5
  222.3 93.2 %copy-start.10 = (f32[56,128]{1,0:T(8,128)S(1)}, f32[56,128]{1,0:T(8,128)}, u32[]{:S(2)}) copy-start(f32[56,128]{1,0:T(8,128)} %copy-done.9) | copy-start | bytes 86020
  241.8 0.9 copy-start.3
  242.8 169.7 %all-reduce.16.cloned.1.call-start = ((), (), s32[]{:S(2)}) async-start(), calls=%async_computation.4 | async-start | bytes 1376256 | tf_op jit(solution)/shard_map/psum | solution.py:212
  316.5 0.7 copy-start.11
  318.5 0.8 copy-start.6
  319.3 20.6 %copy-start.19 = (f32[100]{0:T(128)S(1)}, f32[100]{0:T(128)}, u32[]{:S(2)}) copy-start(f32[100]{0:T(128)} %param.17) | copy-start | bytes 1204
  338.8 0.9 copy-start
  339.7 118.5 %reduce-scatter.4.cloned.1.call-start = ((), (), s32[]{:S(2)}) async-start(), calls=%async_computation.5 | async-start | bytes 2048000
  415.0 3.1 copy-start.8
  417.2 1.7 copy-start.13
Sparse Core Ops, SparseCore 0:
  47.2 76.4 all-reduce.9
  147.1 72.6 all-reduce.11
  242.9 72.6 all-reduce.13
  339.8 72.5 all-reduce.15
  430.6 27.5 reduce-scatter.3

commit v2 on v1

--- a/solution.py
+++ b/solution.py
@@ -116,23 +116,198 @@
     return pack(0) + g_re * den, pack(1) + g_im * den, den
 
 
-def sums_kernel(whole_tiles, g_ref, coh_ref, tail_ref, vis_ref, t1, t2, tt, out_ref, gp, gq, xs):
+MESH = pl.DeviceIdType.MESH
+LAG_B, LAG_C, LAG_D = 2, 4, 6
+
+
+def fused_kernel(
+    whole_tiles, half_k, steps,
+    g0, target, scaled, weight, smooth, coh_hbm, tail, vis, t1, t2, tt,
+    gains_out, cons_out,
+    coh, gfull, cfull, psend, yrecv, zbuf, zrecv, mix, mixrecv, gp, gq, xs,
+    coh_sem, ysend_sem, yrecv_sem, zsend_sem, zrecv_sem, gz_send, gz_recv, gy_send, gy_recv,
+    mix_send, mix_recv, cz_send, cz_recv, cy_send, cy_recv,
+):
+    bands, _, packed, _ = gfull.shape
     rows = t1.shape[1]
-
-    def load_c(kt, rsl):
-        if kt < whole_tiles:
-            return (coh_ref[0, 0, pl.ds(kt * TILE, TILE), rsl], coh_ref[1, 0, pl.ds(kt * TILE, TILE), rsl])
-        sl = pl.ds((kt - whole_tiles) * TILE, TILE)
-        return tail_ref[0, 0, sl, rsl], tail_ref[1, 0, sl, rsl]
-
-    def load_v(rsl):
-        return vis_ref[0, 0, :, rsl], vis_ref[1, 0, :, rsl]
-
-    half_k = out_ref.shape[2]
-    re, im, den = band_sums(g_ref[0, 0], g_ref[0, 1], load_c, load_v, rows, t1, t2, tt, gp, gq, xs)
-    out_ref[0, 0] = re
-    out_ref[0, 1] = im
-    out_ref[0, 2] = den
+    nblk, nband = lax.axis_size("blk"), lax.axis_size("band")
+    nz = nblk // 2
+    piece = packed // nblk
+    half = packed // 2
+    me = lax.axis_index("blk")
+    group = lax.axis_index("band")
+    y, z = lax.rem(me, 2), me // 2
+    partner = {"blk": z * 2 + (1 - y)}
+
+    def peer(d):
+        return {"blk": lax.rem(z + d, nz) * 2 + y}
+
+    def band_peer(d):
+        return {"band": lax.rem(group + d, nband)}
+
+    def span(start, size):
+        return pl.ds(pl.multiple_of(start, 8), size)
+
+    def piece_of(zi):
+        return span(y * half + zi * piece, piece)
+
+    own = piece_of(z)
+    own_half = span(y * half, half)
+    other_half = span((1 - y) * half, half)
+
+    def remote(src, dst, send, recv, device):
+        return pltpu.make_async_remote_copy(
+            src_ref=src, dst_ref=dst, send_sem=send, recv_sem=recv, device_id=device, device_id_type=MESH
+        )
+
+    def coh_copy(f):
+        return pltpu.make_async_copy(coh_hbm.at[:, f], coh.at[f], coh_sem.at[f])
+
+    def y_copy(f):
+        return remote(psend.at[f, :, other_half], yrecv.at[f], ysend_sem.at[f], yrecv_sem.at[f], partner)
+
+    def z_copy(f, d):
+        where = span(lax.rem(z + d, nz) * piece, piece)
+        return remote(zbuf.at[f, :, where], zrecv.at[f, d - 1], zsend_sem.at[f, d - 1], zrecv_sem.at[f, d - 1], peer(d))
+
+    def all_z(buf, send, recv, f, d, incoming):
+        where = piece_of(lax.rem(z + nz - d, nz)) if incoming else own
+        return remote(buf.at[f, :, where], buf.at[f, :, where], send.at[f, d - 1], recv.at[f, d - 1], peer(d))
+
+    def all_y(buf, send, recv, f, incoming):
+        where = other_half if incoming else own_half
+        return remote(buf.at[f, :, where], buf.at[f, :, where], send.at[f], recv.at[f], partner)
+
+    def mix_copy(f, d):
+        return remote(mix.at[f], mixrecv.at[d - 1, f], mix_send.at[f, d - 1], mix_recv.at[f, d - 1], band_peer(d))
+
+    for f in range(bands):
+        coh_copy(f).start()
+    barrier = pltpu.get_barrier_semaphore()
+    pl.semaphore_signal(barrier, inc=1, device_id=partner, device_id_type=MESH)
+    for d in range(1, nz):
+        pl.semaphore_signal(barrier, inc=1, device_id=peer(d), device_id_type=MESH)
+    for d in range(1, nband):
+        pl.semaphore_signal(barrier, inc=1, device_id=band_peer(d), device_id_type=MESH)
+    gfull[...] = g0[...]
+    psend[...] = jnp.zeros_like(psend)
+    pl.semaphore_wait(barrier, nz + nband - 1)
+
+    def compute(n):
+        f = lax.rem(n, bands)
+
+        @pl.when(n < bands)
+        def _():
+            coh_copy(f).wait()
+
+        @pl.when(n >= bands)
+        def _():
+            all_y(gfull, gy_send, gy_recv, f, False).wait_send()
+            all_y(gfull, gy_send, gy_recv, f, True).wait_recv()
+
+        def load_c(kt, rsl):
+            if kt < whole_tiles:
+                return (coh[f, 0, pl.ds(kt * TILE, TILE), rsl], coh[f, 1, pl.ds(kt * TILE, TILE), rsl])
+            sl = pl.ds((kt - whole_tiles) * TILE, TILE)
+            return tail[0, f, sl, rsl], tail[1, f, sl, rsl]
+
+        def load_v(rsl):
+            return vis[0, pl.ds(f, 1), rsl], vis[1, pl.ds(f, 1), rsl]
+
+        g_re, g_im = gfull[f, 0, :half_k], gfull[f, 1, :half_k]
+        sums = band_sums(g_re, g_im, load_c, load_v, rows, t1, t2, tt, gp, gq, xs)
+        for i in range(3):
+            psend[f, i, :half_k] = sums[i]
+        y_copy(f).start()
+
+    def stage_b(n):
+        f = lax.rem(n, bands)
+        y_copy(f).wait()
+        zbuf[f] = psend[f, :, own_half] + yrecv[f]
+        for d in range(1, nz):
+            z_copy(f, d).start()
+
+    def stage_c(n):
+        f = lax.rem(n, bands)
+        total = zbuf[f, :, span(z * piece, piece)]
+        for d in range(1, nz):
+            z_copy(f, d).wait()
+            total = total + zrecv[f, d - 1]
+        w = weight[own]
+        inverse = 0.5 / (total[2] + w)
+        for c in range(2):
+            fresh = (total[c] + w * target[f, c, own]) * inverse
+            value = 0.5 * gfull[f, c, own] + fresh
+            gfull[f, c, own] = value
+            mix[f, c] = value + scaled[f, c, own]
+        for d in range(1, nz):
+            all_z(gfull, gz_send, gz_recv, f, d, False).start()
+
+        @pl.when(n >= steps - bands)
+        def _():
+            for d in range(1, nband):
+                mix_copy(f, d).start()
+
+    def stage_d(n):
+        f = lax.rem(n, bands)
+        for d in range(1, nz):
+            all_z(gfull, gz_send, gz_recv, f, d, False).wait_send()
+            all_z(gfull, gz_send, gz_recv, f, d, True).wait_recv()
+        all_y(gfull, gy_send, gy_recv, f, False).start()
+
+    def turn(n, carry):
+        @pl.when(n < steps)
+        def _():
+            compute(n)
+
+        for lag, stage in ((LAG_B, stage_b), (LAG_C, stage_c), (LAG_D, stage_d)):
+            @pl.when(jnp.logical_and(n >= lag, n < steps + lag))
+            def _(lag=lag, stage=stage):
+                stage(n - lag)
+
+        return carry
+
+    lax.fori_loop(0, steps + LAG_D, turn, 0)
+
+    for d in range(1, nband):
+        for f in range(bands):
+            mix_copy(f, d).wait()
+
+    def smooth_band(f, carry):
+        acc = [jnp.zeros((piece, LANES), jnp.float32) for _ in range(2)]
+        for d in range(nband):
+            source = lax.rem(group + nband - d, nband)
+            for h in range(bands):
+                w = smooth[f, source * bands + h]
+                for c in range(2):
+                    acc[c] += w * (mix[h, c] if d == 0 else mixrecv[d - 1, h, c])
+        for c in range(2):
+            cfull[f, c, own] = acc[c]
+        for d in range(1, nz):
+            all_z(cfull, cz_send, cz_recv, f, d, False).start()
+        return carry
+
+    lax.fori_loop(0, bands, smooth_band, 0)
+
+    def spread_y(f, carry):
+        for d in range(1, nz):
+            all_z(cfull, cz_send, cz_recv, f, d, False).wait_send()
+            all_z(cfull, cz_send, cz_recv, f, d, True).wait_recv()
+        all_y(cfull, cy_send, cy_recv, f, False).start()
+        return carry
+
+    lax.fori_loop(0, bands, spread_y, 0)
+
+    def finish(f, carry):
+        all_y(gfull, gy_send, gy_recv, f, False).wait_send()
+        all_y(gfull, gy_send, gy_recv, f, True).wait_recv()
+        gains_out[f] = gfull[f]
+        all_y(cfull, cy_send, cy_recv, f, False).wait_send()
+        all_y(cfull, cy_send, cy_recv, f, True).wait_recv()
+        cons_out[f] = cfull[f]
+        return carry
+
+    lax.fori_loop(0, bands, finish, 0)
 
 
 def tables(station_first, station_second):
@@ -146,17 +321,18 @@
     return gather_table(station_first), gather_table(station_second), spread
 
 
-def packer(stations, bands, directions, half_k):
-    def pack(x, fill=0.0):
+def packer(stations, bands, directions, half_k, packed):
+    def pack(x):
         c = x.shape[0]
         x = x.reshape(c, x.shape[1], bands, directions)
-        x = jnp.pad(x, ((0, 0), (0, HALF - x.shape[1]), (0, 0), (0, 2 * half_k - directions)), constant_values=fill)
+        x = jnp.pad(x, ((0, 0), (0, HALF - x.shape[1]), (0, 0), (0, 2 * half_k - directions)))
         x = x.reshape(c, HALF, bands, 2, half_k).transpose(2, 0, 4, 3, 1)
-        return x.reshape(bands, c, half_k, LANES)
+        x = x.reshape(bands, c, half_k, LANES)
+        return jnp.pad(x, ((0, 0), (0, 0), (0, packed - half_k), (0, 0)))
 
     def unpack(x):
         c = x.shape[1]
-        x = x.reshape(bands, c, half_k, 2, HALF).transpose(1, 4, 0, 3, 2)
+        x = x[:, :, :half_k].reshape(bands, c, half_k, 2, HALF).transpose(1, 4, 0, 3, 2)
         x = x.reshape(c, HALF, bands, 2 * half_k)[:, :stations, :, :directions]
         return x.reshape(c, stations, bands * directions)
 
@@ -169,58 +345,67 @@
     bands = visibility.shape[1]
     rows = visibility.shape[2]
     groups = lax.axis_size("blk")
-    bands_all = bands * lax.axis_size("band")
+    nband = lax.axis_size("band")
+    bands_all = bands * nband
     full_k = round_up(directions, TILE)
     half_k = full_k // 2
+    packed = round_up(half_k, 8 * groups)
+    piece = packed // groups
+    nz = groups // 2
     whole_tiles = directions // TILE
     t1, t2, tt = tables(station_first, station_second)
     tail = jnp.pad(coherency[:, :, whole_tiles * TILE :, :], ((0, 0), (0, 0), (0, full_k - directions), (0, 0)))
     tail = tail if full_k > whole_tiles * TILE else coherency[:, :, :TILE, :]
-    pack, unpack = packer(stations, bands, directions, half_k)
+    pack, unpack = packer(stations, bands, directions, half_k, packed)
     rho_col = jnp.tile(penalty, bands)
     scaled = dual_prev / rho_col
-    target = pack(consensus_prev - scaled)
     rho_pack = jnp.pad(penalty, (0, full_k - directions), constant_values=1.0).reshape(2, half_k).T
+    rho_pack = jnp.pad(rho_pack, ((0, packed - half_k), (0, 0)), constant_values=1.0)
     weight = jnp.repeat(rho_pack * (rows * groups / (stations * directions)), HALF, axis=1)
-    gains = pack(gains_start)
-    vis = visibility[:, :, None, :]
-    whole = lambda f: (0, 0)
-    call = pl.pallas_call(
-        functools.partial(sums_kernel, whole_tiles),
-        out_shape=jax.ShapeDtypeStruct((bands, 3, half_k, LANES), jnp.float32),
-        grid=(bands,),
-        in_specs=[
-            pl.BlockSpec((1, 2, half_k, LANES), lambda f: (f, 0, 0, 0)),
-            pl.BlockSpec((2, 1, directions, rows), lambda f: (0, f, 0, 0)),
-            pl.BlockSpec((2, 1, tail.shape[2], rows), lambda f: (0, f, 0, 0)),
-            pl.BlockSpec((2, 1, 1, rows), lambda f: (0, f, 0, 0)),
-            pl.BlockSpec((LANES, rows), whole),
-            pl.BlockSpec((LANES, rows), whole),
-            pl.BlockSpec((rows // CHUNK, 4 * CHUNK, LANES), lambda f: (0, 0, 0)),
+    solved = smoother(noise_var, bands_all)[:, :, :full_k]
+    solved = lax.dynamic_slice_in_dim(solved, lax.axis_index("band") * bands, bands, 1)
+    solved = solved.reshape(bands_all, bands, 2, half_k)
+    solved = jnp.pad(solved, ((0, 0), (0, 0), (0, 0), (0, packed - half_k)))
+    me = lax.axis_index("blk")
+    position = (me % 2) * (packed // 2) + (me // 2) * piece
+    solved = lax.dynamic_slice_in_dim(solved, position, piece, 3).transpose(1, 0, 3, 2)
+    smooth = jnp.repeat(solved, HALF, axis=3)
+    vmem = pl.BlockSpec(memory_space=pltpu.VMEM)
+    dma = pltpu.SemaphoreType.DMA
+    full = jax.ShapeDtypeStruct((bands, 2, packed, LANES), jnp.float32)
+    f32 = jnp.float32
+    gains, consensus = pl.pallas_call(
+        functools.partial(fused_kernel, whole_tiles, half_k, ITERS * bands),
+        out_shape=(full, full),
+        in_specs=[vmem] * 5 + [pl.BlockSpec(memory_space=pl.ANY)] + [vmem] * 5,
+        out_specs=(vmem, vmem),
+        scratch_shapes=[
+            pltpu.VMEM((bands, 2, directions, rows), f32),
+            pltpu.VMEM((bands, 2, packed, LANES), f32),
+            pltpu.VMEM((bands, 2, packed, LANES), f32),
+            pltpu.VMEM((bands, 3, packed, LANES), f32),
+            pltpu.VMEM((bands, 3, packed // 2, LANES), f32),
+            pltpu.VMEM((bands, 3, packed // 2, LANES), f32),
+            pltpu.VMEM((bands, nz - 1, 3, piece, LANES), f32),
+            pltpu.VMEM((bands, 2, piece, LANES), f32),
+            pltpu.VMEM((nband - 1, bands, 2, piece, LANES), f32),
+            pltpu.VMEM((2, 2 * full_k, CHUNK), f32),
+            pltpu.VMEM((2, 2 * full_k, CHUNK), f32),
+            pltpu.VMEM((2, 3 * full_k, 4 * CHUNK), jnp.bfloat16),
+            dma((bands,)),
+            dma((bands,)), dma((bands,)),
+            dma((bands, nz - 1)), dma((bands, nz - 1)),
+            dma((bands, nz - 1)), dma((bands, nz - 1)),
+            dma((bands,)), dma((bands,)),
+            dma((bands, nband - 1)), dma((bands, nband - 1)),
+            dma((bands, nz - 1)), dma((bands, nz - 1)),
+            dma((bands,)), dma((bands,)),
         ],
-        out_specs=pl.BlockSpec((1, 3, half_k, LANES), lambda f: (f, 0, 0, 0)),
-        scratch_shapes=[
-            pltpu.VMEM((2, 2 * full_k, CHUNK), jnp.float32),
-            pltpu.VMEM((2, 2 * full_k, CHUNK), jnp.float32),
-            pltpu.VMEM((2, 3 * full_k, 4 * CHUNK), jnp.bfloat16),
-        ],
-        compiler_params=pltpu.CompilerParams(vmem_limit_bytes=48 << 20),
-        name="band_sums",
-    )
-    for step in range(ITERS):
-        parts = call(gains, coherency, tail, vis, t1, t2, tt)
-        total = lax.psum(parts, "blk")
-        fresh = (total[:, :2] + weight * target) / (total[:, 2:] + weight)
-        gains = 0.5 * gains + 0.5 * fresh
+        compiler_params=pltpu.CompilerParams(collective_id=0, has_side_effects=True, vmem_limit_bytes=56 << 20),
+        name="admm",
+    )(pack(gains_start), pack(consensus_prev - scaled), pack(scaled), weight, smooth, coherency, tail, visibility, t1, t2, tt)
     gains = unpack(gains)
-    mixed = gains + scaled
-    smooth = smoother(noise_var, bands_all)[:, :, :directions]
-    offset = lax.axis_index("band") * bands
-    cols = lax.dynamic_slice_in_dim(smooth, offset, bands, 0)
-    local_view = mixed.reshape(2, stations, bands, directions)
-    term = jnp.einsum("gfk,cpgk->cpfk", cols, local_view, precision=lax.Precision.HIGHEST)
-    term = term.reshape(2, stations, bands_all * directions)
-    consensus = lax.psum_scatter(term, "band", scatter_dimension=2, tiled=True)
+    consensus = unpack(consensus)
     dual = dual_prev + rho_col * (gains - consensus)
     return (gains, consensus, dual)
 

time: 471 us -> 177 us (0.38)
  waiting for transfers between devices: 300 us -> 0 us
  Pallas kernels: 83.3 us -> 128 us
  between operations: 14.3 us -> 1.04 us
  local copies, waits for them, and re-layouts: 56.7 us -> 43.6 us
  other arithmetic: 12.5 us -> 3.86 us
    psum x4 -> x0, waiting for transfers between devices: 273 us -> none  [on_device(): total = lax.psum(parts, 'blk')]
    pallas_call x4 -> x1, Pallas kernels: 77.9 us -> 122 us  [on_device(): pl.pallas_call(functools.partial(fused_kernel, whole_tiles, half_k, ITERS...]
    unnamed x6 -> x0, waiting for transfers between devices: 26.7 us -> none
    unnamed x49 -> x27, local copies, waits for them, and re-layouts: 30 us -> 12 us
    add x5 -> x0, other arithmetic: 5.65 us -> none  [the longest x4 5.59 us: on_device(): gains = 0.5 * gains + 0.5 * fresh]
  transfers between devices with their start and end apart: 5 -> 0, of which waited for: 5 -> 0; matrix products, arithmetic and copies ran while one was open for 4% -> 0% of each run, Pallas kernels for 1% -> 0%
where the time goes in v2:
time: 177 us; the launch traced here: 176 us
  Pallas kernels  128 us (72%)
  local copies, waits for them, and re-layouts  43.6 us (25%)
  other arithmetic  3.86 us (2%)
    pallas_call x1, Pallas kernels, on_device(): pl.pallas_call(functools.partial(fused_kernel, whole_tiles, half_k, ITERS...  122 us
    unnamed x27, local copies, waits for them, and re-layouts  12 us
    pallas_call x1, Pallas kernels, smoother(): pl.pallas_call(functools.partial(smoother_kernel, count), out_shape=jax.S...  5.42 us
    transpose x3, local copies, waits for them, and re-layouts, pack(): x = x.reshape(c, HALF, bands, 2, half_k).transpose(2, 0, 4, 3, 1)  4.97 us
    reshape x4, local copies, waits for them, and re-layouts, unpack(): x[:, :, :half_k].reshape(bands, c, half_k, 2, HALF).transpose(1, 4, 0, 3, 2)  4.47 us

profile of v2, /device:TPU:0, one launch (start us, length us, event | category | flops | bytes accessed | tf_op | source)
XLA Modules:
  0.0 176.2 jit_solution(11738489274522756117)
XLA Ops:
  0.7 0.7 pad_bitcast_fusion.noise_ref
  1.3 0.7 pad.46
  2.0 0.1 reshape.114
  2.1 0.7 tile.2
  2.8 0.8 add_bitcast_fusion
  3.6 0.1 copy.53
  3.7 0.1 broadcast_in_dim.11
  3.9 0.7 reshape.115.weight
  4.6 1.5 reshape.105
  6.2 5.4 %smoother.1 = f32[32,32,128]{2,1,0:T(8,128)S(1)} custom-call(f32[1,128]{1,0:T(1,128)S(1)} %pad_bitcast_fusion.noise_ref), custom_call_target="tpu_custom_call" | custom-call | tf_op jit(solution)/shard_map/smoother/pallas_call | solution.py:45
  11.7 0.2 reshape.116
  11.9 0.3 dynamic-slice_bitcast_fusion
  12.2 0.6 reshape.106
  12.9 1.7 copy.48
  14.6 0.5 reshape.107
  15.1 0.9 pad.41.g0
  15.9 0.9 compare_convert_fusion.1
  16.9 1.6 copy.54
  18.5 0.3 reshape.111
  18.9 0.3 reshape.108
  19.2 0.6 reshape.109
  19.8 1.7 copy.51
  21.5 0.5 reshape.110
  22.0 0.9 pad.43.target
  22.8 0.6 reshape.112
  23.5 1.7 copy.52
  25.1 0.5 reshape.113
  25.6 0.8 pad.45.scaled
  26.5 2.0 %compare_convert_fusion.tt = bf16[4,1024,128]{2,1,0:T(8,128)(2,1)} fusion(s32[128]{0:T(128)S(1)} %copy-done.10, s32[4,1024]{1,0:T(4,128)S(1)} %bitcast.38), kind=kLoop, calls=%fused_computation | loop fusion | flops 1048576 | bytes 1065472 | tf_op jit(solution)/shard_map/convert_element_type | solution.py:320
  28.5 2.6 %broadcast_in_dim.13 = f32[8,32,8,2,64]{4,3,2,1,0:T(2,128)S(1)} broadcast(f32[8,32,8,2]{3,2,1,0:T(8,128)S(1)} %copy.54), dimensions={0,1,2,3} | broadcast | bytes 1064960 | tf_op jit(solution)/shard_map/broadcast_in_dim | solution.py:372
  31.1 2.1 %reshape.117.smooth = f32[8,32,8,128]{3,2,1,0:T(8,128)} reshape(f32[8,32,8,2,64]{4,3,2,1,0:T(2,128)S(1)} %broadcast_in_dim.13) | data formatting | bytes 2097152 | tf_op jit(solution)/shard_map/reshape | solution.py:372
  33.2 6.7 %copy.56.coh_hbm = f32[2,8,100,1024]{3,2,1,0:T(8,128)S(1)} copy(f32[2,8,100,1024]{3,1,2,0:T(8,128)} %param.10) | data formatting | bytes 13107200 | tf_op args[1]
  39.9 1.3 pad.50.tail
  41.2 1.8 %copy-done = f32[2,8,100,1024]{3,2,1,0:T(8,128)} copy-done((f32[2,8,100,1024]{3,2,1,0:T(8,128)}, f32[2,8,100,1024]{3,2,1,0:T(8,128)S(1)}, u32[]{:S(2)}) %copy-start) | copy-done | bytes 6553624
  43.0 122.3 %admm.1 = (f32[8,2,64,128]{3,2,1,0:T(8,128)}, f32[8,2,64,128]{3,2,1,0:T(8,128)}) custom-call(f32[8,2,64,128]{3,2,1,0:T(8,128)} %pad.41.g0, f32[8,2,64,128]{3,2,1,0:T(8,128)} %pad.43.target, f32[8,2,64,128]{3,2,1,0:T(8,128)} %pad.45.scaled, f32[64,128]{1,0:T(8,128)} %reshape.115.weight, f32[8,32,8,128]{3,2,1,0:T(8,128)} %reshape.117.smooth, ...), custom_call_target="tpu_custom_call" | custom-call | tf_op jit(solution)/shard_map/admm/pallas_call | solution.py:377
  165.4 1.1 slice.20
  166.4 0.5 reshape.120
  167.0 1.7 copy.57
  168.7 0.6 reshape.121
  169.3 0.2 reshape.122
  169.5 1.1 copy.60
  170.7 0.5 reshape.123
  171.2 1.7 copy.58
  172.9 0.6 reshape.124
  173.6 0.2 reshape.125
  173.8 0.2 copy-done.2
  174.0 1.1 copy.61
  175.1 1.1 copy.62
  (35 shorter events, 0.6 us)
Async XLA Ops:
  0.7 15.3 %copy-start.9 = (s32[128]{0:T(128)}, s32[128]{0:T(128)S(1)}, u32[]{:S(2)}) copy-start(s32[128]{0:T(128)S(1)} %and_select_fusion) | copy-start | bytes 1540
  2.8 15.6 %copy-start.5 = (f32[800]{0:T(1024)}, f32[800]{0:T(1024)S(1)}, u32[]{:S(2)}) copy-start(f32[800]{0:T(1024)S(1)} %div.18) | copy-start | bytes 9604
  12.8 3.1 %copy-start.7 = (s32[1024]{0:T(1024)S(1)}, s32[1024]{0:T(1024)}, u32[]{:S(2)}) copy-start(s32[1024]{0:T(1024)} %param.12) | copy-start | bytes 12292
  12.9 3.1 %copy-start.8 = (s32[1024]{0:T(1024)S(1)}, s32[1024]{0:T(1024)}, u32[]{:S(2)}) copy-start(s32[1024]{0:T(1024)} %param.11) | copy-start | bytes 12292
  14.5 3.9 %copy-start.1 = (f32[2,62,800]{2,0,1:T(2,128)S(1)}, f32[2,62,800]{2,0,1:T(2,128)}, u32[]{:S(2)}) copy-start(f32[2,62,800]{2,0,1:T(2,128)} %param.15) | copy-start | bytes 1190404
  14.5 3.9 %copy-start.3 = (f32[2,62,800]{2,0,1:T(2,128)S(1)}, f32[2,62,800]{2,0,1:T(2,128)}, u32[]{:S(2)}) copy-start(f32[2,62,800]{2,0,1:T(2,128)} %param.14) | copy-start | bytes 1190404
  23.5 3.0 %copy-start.10 = (s32[128]{0:T(128)S(1)}, s32[128]{0:T(128)}, u32[]{:S(2)}) copy-start(s32[128]{0:T(128)} %copy-done.9) | copy-start | bytes 1540
  39.9 3.1 %copy-start = (f32[2,8,100,1024]{3,2,1,0:T(8,128)}, f32[2,8,100,1024]{3,2,1,0:T(8,128)S(1)}, u32[]{:S(2)}) copy-start(f32[2,8,100,1024]{3,2,1,0:T(8,128)S(1)} %copy.56.coh_hbm) | copy-start | bytes 19660804
  168.7 2.0 %copy-start.4 = (f32[8,2,64,128]{3,2,1,0:T(8,128)S(1)}, f32[8,2,64,128]{3,2,1,0:T(8,128)}, u32[]{:S(2)}) copy-start(f32[8,2,64,128]{3,2,1,0:T(8,128)} %get-tuple-element.6) | copy-start | bytes 1572868
  172.9 1.0 copy-start.2
  172.9 1.0 copy-start.6

commit v3 on v2

--- a/solution.py
+++ b/solution.py
@@ -17,41 +17,60 @@
     return (x + m - 1) // m * m
 
 
-def smoother_kernel(count, noise_ref, out_ref, work):
-    level = noise_ref[...]
-    cols = lax.broadcasted_iota(jnp.int32, (count, LANES), 0)
+def invert(count, level, work):
+    lanes = level.shape[1]
+    cols = lax.broadcasted_iota(jnp.int32, (count, lanes), 0)
     for i in range(count):
         diff = (cols - i).astype(jnp.float32) / (count / 4.0)
-        kern = jnp.exp(-0.5 * diff * diff)
-        work[i, :count, :] = kern + jnp.where(cols == i, level, 0.0)
-        work[i, count:, :] = kern
+        work[i] = jnp.exp(-0.5 * diff * diff) + jnp.where(cols == i, level, 0.0)
 
     def eliminate(p, carry):
-        pivot = work[p, pl.ds(p, 1), :]
-        row = work[p] / pivot
+        inverse = 1.0 / work[p, pl.ds(p, 1), :]
+        at = cols == p
+        row = jnp.where(at, 1.0, work[p]) * inverse
         for i in range(count):
-            work[i] = work[i] - work[i, pl.ds(p, 1), :] * row
+            factor = work[i, pl.ds(p, 1), :]
+            work[i] = jnp.where(at, 0.0, work[i]) - factor * row
         work[p] = row
         return carry
 
     lax.fori_loop(0, count, eliminate, 0)
-    for i in range(count):
-        out_ref[i] = work[i, count:, :]
-
-
-def smoother(noise, count):
-    pad = jnp.pad(noise, (0, LANES * ((noise.shape[0] + LANES - 1) // LANES) - noise.shape[0]), constant_values=1.0)
-    groups = pad.shape[0] // LANES
-    return pl.pallas_call(
-        functools.partial(smoother_kernel, count),
-        out_shape=jax.ShapeDtypeStruct((count, count, groups * LANES), jnp.float32),
-        grid=(groups,),
-        in_specs=[pl.BlockSpec((1, LANES), lambda g: (0, g))],
-        out_specs=pl.BlockSpec((count, count, LANES), lambda g: (0, 0, g)),
-        scratch_shapes=[pltpu.VMEM((count, 2 * count, LANES), jnp.float32)],
-        compiler_params=pltpu.CompilerParams(vmem_limit_bytes=16 << 20),
-        name="smoother",
-    )(pad[None, :])
+
+
+def arrange_smoother(level, work, smooth, first_band, position, half_k):
+    bands, count, piece, _ = smooth.shape
+    lanes = level.shape[1]
+    cols = lax.broadcasted_iota(jnp.int32, (count, lanes), 0)
+    mats = []
+    for f in range(bands):
+        eye = jnp.where(cols == first_band + f, 1.0, 0.0)
+        mats.append(eye - level * work[first_band + f])
+    mats = jnp.concatenate(mats, axis=0)
+    hi = mats.astype(jnp.bfloat16)
+    rest = mats - hi.astype(jnp.float32)
+    mid = rest.astype(jnp.bfloat16)
+    low = (rest - mid.astype(jnp.float32)).astype(jnp.bfloat16)
+    direction = lax.broadcasted_iota(jnp.int32, (lanes, LANES), 0)
+    lane = lax.broadcasted_iota(jnp.int32, (lanes, LANES), 1)
+    for j in range(piece):
+        wanted = jnp.where(lane < HALF, 0, half_k) + position + j
+        pick = jnp.where(direction == wanted, 1.0, 0.0).astype(jnp.bfloat16)
+        rows = sum(jnp.dot(x, pick, preferred_element_type=jnp.float32) for x in (hi, mid, low))
+        for f in range(bands):
+            smooth[f, :, j, :] = rows[f * count : (f + 1) * count]
+
+
+def build_tables(first, second, t1, t2, tt):
+    rows = t1.shape[1]
+    slot = lax.rem(lax.broadcasted_iota(jnp.int32, (LANES, CHUNK), 0), HALF)
+    for rc in range(rows // CHUNK):
+        rsl = pl.ds(rc * CHUNK, CHUNK)
+        for side, (stations, table) in enumerate(((first, t1), (second, t2))):
+            hot = jnp.where(slot == stations[:, rsl], 1.0, 0.0)
+            table[:, rsl] = hot.astype(jnp.bfloat16)
+            turned = jnp.transpose(hot).astype(jnp.bfloat16)
+            for part in range(2):
+                tt[rc, pl.ds((2 * side + part) * CHUNK, CHUNK), :] = turned
 
 
 def band_sums(g_re, g_im, load_c, load_v, rows, t1, t2, tt, gp, gq, xs):
@@ -67,11 +86,18 @@
             parts.append(jnp.where(low, hi, full - hi))
     lhs = jnp.concatenate(parts, axis=0).astype(jnp.bfloat16)
     total = None
+
+    def gather(rc):
+        rsl = pl.ds(rc * CHUNK, CHUNK)
+        gp[rc % 2] = jnp.dot(lhs, t1[:, rsl], preferred_element_type=jnp.float32)
+        gq[rc % 2] = jnp.dot(lhs, t2[:, rsl], preferred_element_type=jnp.float32)
+
+    gather(0)
     for rc in range(rows // CHUNK):
         buf = rc % 2
         rsl = pl.ds(rc * CHUNK, CHUNK)
-        gp[buf] = jnp.dot(lhs, t1[:, rsl], preferred_element_type=jnp.float32)
-        gq[buf] = jnp.dot(lhs, t2[:, rsl], preferred_element_type=jnp.float32)
+        if rc + 1 < rows // CHUNK:
+            gather(rc + 1)
         sum_re = jnp.zeros((TILE, CHUNK), jnp.float32)
         sum_im = jnp.zeros((TILE, CHUNK), jnp.float32)
 
@@ -121,14 +147,16 @@
 
 
 def fused_kernel(
-    whole_tiles, half_k, steps,
-    g0, target, scaled, weight, smooth, coh_hbm, tail, vis, t1, t2, tt,
-    gains_out, cons_out,
-    coh, gfull, cfull, psend, yrecv, zbuf, zrecv, mix, mixrecv, gp, gq, xs,
+    half_k, steps, weight_per_rho,
+    state, rho, noise, coh_hbm, vis, first, second,
+    out,
+    t1, t2, tt, work, smooth, coh, tail, gfull, cfull, psend, yrecv, zbuf, zrecv, mix, mixrecv, gp, gq, xs,
     coh_sem, ysend_sem, yrecv_sem, zsend_sem, zrecv_sem, gz_send, gz_recv, gy_send, gy_recv,
     mix_send, mix_recv, cz_send, cz_recv, cy_send, cy_recv,
 ):
     bands, _, packed, _ = gfull.shape
+    directions = coh_hbm.shape[1]
+    whole = directions // TILE * TILE
     rows = t1.shape[1]
     nblk, nband = lax.axis_size("blk"), lax.axis_size("band")
     nz = nblk // 2
@@ -161,7 +189,7 @@
         )
 
     def coh_copy(f):
-        return pltpu.make_async_copy(coh_hbm.at[:, f], coh.at[f], coh_sem.at[f])
+        return pltpu.make_async_copy(coh_hbm.at[:, :, f], coh.at[f], coh_sem.at[f])
 
     def y_copy(f):
         return remote(psend.at[f, :, other_half], yrecv.at[f], ysend_sem.at[f], yrecv_sem.at[f], partner)
@@ -189,8 +217,10 @@
         pl.semaphore_signal(barrier, inc=1, device_id=peer(d), device_id_type=MESH)
     for d in range(1, nband):
         pl.semaphore_signal(barrier, inc=1, device_id=band_peer(d), device_id_type=MESH)
-    gfull[...] = g0[...]
+    gfull[...] = state[:, 0:2]
     psend[...] = jnp.zeros_like(psend)
+    tail[...] = jnp.zeros_like(tail)
+    build_tables(first, second, t1, t2, tt)
     pl.semaphore_wait(barrier, nz + nband - 1)
 
     def compute(n):
@@ -199,6 +229,9 @@
         @pl.when(n < bands)
         def _():
             coh_copy(f).wait()
+            if directions > whole:
+                for c in range(2):
+                    tail[f, c, : directions - whole] = coh[f, c, whole:]
 
         @pl.when(n >= bands)
         def _():
@@ -206,10 +239,10 @@
             all_y(gfull, gy_send, gy_recv, f, True).wait_recv()
 
         def load_c(kt, rsl):
-            if kt < whole_tiles:
-                return (coh[f, 0, pl.ds(kt * TILE, TILE), rsl], coh[f, 1, pl.ds(kt * TILE, TILE), rsl])
-            sl = pl.ds((kt - whole_tiles) * TILE, TILE)
-            return tail[0, f, sl, rsl], tail[1, f, sl, rsl]
+            if kt * TILE < whole:
+                sl = pl.ds(kt * TILE, TILE)
+                return coh[f, 0, sl, rsl], coh[f, 1, sl, rsl]
+            return tail[f, 0, :, rsl], tail[f, 1, :, rsl]
 
         def load_v(rsl):
             return vis[0, pl.ds(f, 1), rsl], vis[1, pl.ds(f, 1), rsl]
@@ -233,13 +266,14 @@
         for d in range(1, nz):
             z_copy(f, d).wait()
             total = total + zrecv[f, d - 1]
-        w = weight[own]
+        w = rho[own] * weight_per_rho
         inverse = 0.5 / (total[2] + w)
         for c in range(2):
-            fresh = (total[c] + w * target[f, c, own]) * inverse
+            scaled = state[f, 4 + c, own] / rho[own]
+            fresh = (total[c] + w * (state[f, 2 + c, own] - scaled)) * inverse
             value = 0.5 * gfull[f, c, own] + fresh
             gfull[f, c, own] = value
-            mix[f, c] = value + scaled[f, c, own]
+            mix[f, c] = value + scaled
         for d in range(1, nz):
             all_z(gfull, gz_send, gz_recv, f, d, False).start()
 
@@ -265,10 +299,15 @@
             def _(lag=lag, stage=stage):
                 stage(n - lag)
 
+        @pl.when(n == steps + LAG_B - 1)
+        def _():
+            invert(smooth.shape[1], noise[...], work)
+
         return carry
 
     lax.fori_loop(0, steps + LAG_D, turn, 0)
 
+    arrange_smoother(noise[...], work, smooth, group * bands, y * half + z * piece, half_k)
     for d in range(1, nband):
         for f in range(bands):
             mix_copy(f, d).wait()
@@ -301,24 +340,16 @@
     def finish(f, carry):
         all_y(gfull, gy_send, gy_recv, f, False).wait_send()
         all_y(gfull, gy_send, gy_recv, f, True).wait_recv()
-        gains_out[f] = gfull[f]
         all_y(cfull, cy_send, cy_recv, f, False).wait_send()
         all_y(cfull, cy_send, cy_recv, f, True).wait_recv()
-        cons_out[f] = cfull[f]
+        for c in range(2):
+            g, cons = gfull[f, c], cfull[f, c]
+            out[f, c] = g
+            out[f, 2 + c] = cons
+            out[f, 4 + c] = state[f, 4 + c] + rho[...] * (g - cons)
         return carry
 
     lax.fori_loop(0, bands, finish, 0)
-
-
-def tables(station_first, station_second):
-    def gather_table(station):
-        return (lax.broadcasted_iota(jnp.int32, (LANES, 1), 0) % HALF == station[None, :]).astype(jnp.bfloat16)
-
-    first = station_first.reshape(-1, 1, CHUNK)
-    second = station_second.reshape(-1, 1, CHUNK)
-    both = jnp.concatenate([first, first, second, second], axis=1).reshape(first.shape[0], 4 * CHUNK, 1)
-    spread = (both == lax.broadcasted_iota(jnp.int32, (1, 1, LANES), 2) % HALF).astype(jnp.bfloat16)
-    return gather_table(station_first), gather_table(station_second), spread
 
 
 def packer(stations, bands, directions, half_k, packed):
@@ -352,35 +383,29 @@
     packed = round_up(half_k, 8 * groups)
     piece = packed // groups
     nz = groups // 2
-    whole_tiles = directions // TILE
-    t1, t2, tt = tables(station_first, station_second)
-    tail = jnp.pad(coherency[:, :, whole_tiles * TILE :, :], ((0, 0), (0, 0), (0, full_k - directions), (0, 0)))
-    tail = tail if full_k > whole_tiles * TILE else coherency[:, :, :TILE, :]
     pack, unpack = packer(stations, bands, directions, half_k, packed)
-    rho_col = jnp.tile(penalty, bands)
-    scaled = dual_prev / rho_col
-    rho_pack = jnp.pad(penalty, (0, full_k - directions), constant_values=1.0).reshape(2, half_k).T
-    rho_pack = jnp.pad(rho_pack, ((0, packed - half_k), (0, 0)), constant_values=1.0)
-    weight = jnp.repeat(rho_pack * (rows * groups / (stations * directions)), HALF, axis=1)
-    solved = smoother(noise_var, bands_all)[:, :, :full_k]
-    solved = lax.dynamic_slice_in_dim(solved, lax.axis_index("band") * bands, bands, 1)
-    solved = solved.reshape(bands_all, bands, 2, half_k)
-    solved = jnp.pad(solved, ((0, 0), (0, 0), (0, 0), (0, packed - half_k)))
-    me = lax.axis_index("blk")
-    position = (me % 2) * (packed // 2) + (me // 2) * piece
-    solved = lax.dynamic_slice_in_dim(solved, position, piece, 3).transpose(1, 0, 3, 2)
-    smooth = jnp.repeat(solved, HALF, axis=3)
+    rho = jnp.pad(penalty, (0, full_k - directions), constant_values=1.0).reshape(2, half_k).T
+    rho = jnp.pad(rho, ((0, packed - half_k), (0, 0)), constant_values=1.0)
+    rho = jnp.repeat(rho, HALF, axis=1)
+    lanes = round_up(full_k, LANES)
+    noise = jnp.pad(noise_var, (0, lanes - directions), constant_values=1.0)[None, :]
+    state = pack(jnp.concatenate([gains_start, consensus_prev, dual_prev], axis=0))
     vmem = pl.BlockSpec(memory_space=pltpu.VMEM)
     dma = pltpu.SemaphoreType.DMA
-    full = jax.ShapeDtypeStruct((bands, 2, packed, LANES), jnp.float32)
-    f32 = jnp.float32
-    gains, consensus = pl.pallas_call(
-        functools.partial(fused_kernel, whole_tiles, half_k, ITERS * bands),
-        out_shape=(full, full),
-        in_specs=[vmem] * 5 + [pl.BlockSpec(memory_space=pl.ANY)] + [vmem] * 5,
-        out_specs=(vmem, vmem),
+    f32, bf16 = jnp.float32, jnp.bfloat16
+    out = pl.pallas_call(
+        functools.partial(fused_kernel, half_k, ITERS * bands, rows * groups / (stations * directions)),
+        out_shape=jax.ShapeDtypeStruct((bands, 6, packed, LANES), f32),
+        in_specs=[vmem] * 3 + [pl.BlockSpec(memory_space=pl.ANY)] + [vmem] * 3,
+        out_specs=vmem,
         scratch_shapes=[
+            pltpu.VMEM((LANES, rows), bf16),
+            pltpu.VMEM((LANES, rows), bf16),
+            pltpu.VMEM((rows // CHUNK, 4 * CHUNK, LANES), bf16),
+            pltpu.VMEM((bands_all, bands_all, lanes), f32),
+            pltpu.VMEM((bands, bands_all, piece, LANES), f32),
             pltpu.VMEM((bands, 2, directions, rows), f32),
+            pltpu.VMEM((bands, 2, TILE, rows), f32),
             pltpu.VMEM((bands, 2, packed, LANES), f32),
             pltpu.VMEM((bands, 2, packed, LANES), f32),
             pltpu.VMEM((bands, 3, packed, LANES), f32),
@@ -391,7 +416,7 @@
             pltpu.VMEM((nband - 1, bands, 2, piece, LANES), f32),
             pltpu.VMEM((2, 2 * full_k, CHUNK), f32),
             pltpu.VMEM((2, 2 * full_k, CHUNK), f32),
-            pltpu.VMEM((2, 3 * full_k, 4 * CHUNK), jnp.bfloat16),
+            pltpu.VMEM((2, 3 * full_k, 4 * CHUNK), bf16),
             dma((bands,)),
             dma((bands,)), dma((bands,)),
             dma((bands, nz - 1)), dma((bands, nz - 1)),
@@ -403,11 +428,9 @@
         ],
         compiler_params=pltpu.CompilerParams(collective_id=0, has_side_effects=True, vmem_limit_bytes=56 << 20),
         name="admm",
-    )(pack(gains_start), pack(consensus_prev - scaled), pack(scaled), weight, smooth, coherency, tail, visibility, t1, t2, tt)
-    gains = unpack(gains)
-    consensus = unpack(consensus)
-    dual = dual_prev + rho_col * (gains - consensus)
-    return (gains, consensus, dual)
+    )(state, rho, noise, coherency.transpose(0, 2, 1, 3), visibility, station_first[None, :], station_second[None, :])
+    out = unpack(out)
+    return (out[0:2], out[2:4], out[4:6])
 
 
 def solution(mesh):

time: 177 us -> 157 us (0.89)
  local copies, waits for them, and re-layouts: 43.6 us -> 33.6 us
  Pallas kernels: 128 us -> 121 us
  other arithmetic: 3.86 us -> 1.87 us
    unnamed x27 -> x8, local copies, waits for them, and re-layouts: 12 us -> 3.43 us
    pallas_call x2 -> x1, Pallas kernels: 128 us -> 121 us  [on_device(): pl.pallas_call(functools.partial(fused_kernel, half_k, ITERS * bands, row...]
    reshape x4 -> x2, local copies, waits for them, and re-layouts: 4.47 us -> 8.46 us  [unpack(): x[:, :, :half_k].reshape(bands, c, half_k, 2, HALF).transpose(1, 4, 0, 3, 2)]
    convert_element_type x2 -> x0, other arithmetic: 2.9 us -> none  [the longest x1 1.96 us: tables(): (both == lax.broadcasted_iota(jnp.int32, (1, 1, LANES), 2) % HALF).astype...]
    reshape x5 -> x1, local copies, waits for them, and re-layouts: 3.48 us -> 0.72 us  [on_device(): rho = jnp.repeat(rho, HALF, axis=1)]
    broadcast_in_dim x3 -> x2, local copies, waits for them, and re-layouts: 3.39 us -> 0.64 us  [the longest x1 0.51 us: on_device(): jnp.pad(noise_var, (0, lanes - directions), constant_values=1.0)[None, :]]
    slice x3 -> x4, local copies, waits for them, and re-layouts: 0.11 us -> 2.09 us  [on_device(): return (out[0:2], out[2:4], out[4:6])]
    transpose x2 -> x0, local copies, waits for them, and re-layouts: 1.9 us -> none  [on_device(): lax.dynamic_slice_in_dim(solved, position, piece, 3).transpose(1, 0, 3, 2)]
where the time goes in v3:
time: 157 us
  Pallas kernels  121 us (77%)
  local copies, waits for them, and re-layouts  33.6 us (21%)
  other arithmetic  1.87 us (1%)
    pallas_call x1, Pallas kernels, on_device(): pl.pallas_call(functools.partial(fused_kernel, half_k, ITERS * bands, row...  121 us
    reshape x2, local copies, waits for them, and re-layouts, unpack(): x[:, :, :half_k].reshape(bands, c, half_k, 2, HALF).transpose(1, 4, 0, 3, 2)  8.46 us
    transpose x1, local copies, waits for them, and re-layouts, pack(): x = x.reshape(c, HALF, bands, 2, half_k).transpose(2, 0, 4, 3, 1)  4.45 us
    unnamed x8, local copies, waits for them, and re-layouts  3.43 us
    reshape x1, local copies, waits for them, and re-layouts, pack(): x = x.reshape(c, HALF, bands, 2, half_k).transpose(2, 0, 4, 3, 1)  3.21 us

profile of v3, /device:TPU:0, one launch (start us, length us, event | category | flops | bytes accessed | tf_op | source)
XLA Modules:
  0.0 156.9 jit_solution(3918865705989527443)
XLA Ops:
  0.6 1.9 %pad_maximum_fusion = f32[6,62,800]{2,0,1:T(8,128)S(1)} fusion(f32[2,62,800]{2,0,1:T(2,128)} %param.15, f32[2,62,800]{2,0,1:T(2,128)} %param.14, f32[2,62,800]{2,0,1:T(2,128)} %param.13), kind=kLoop, calls=%fused_computation | loop fusion | flops 595200 | bytes 2380800 | tf_op jit(solution)/shard_map/concatenate | solution.py:392
  2.5 0.8 reshape.31
  3.3 0.1 copy.20
  3.4 1.3 pad.20
  4.7 3.2 %reshape.32 = f32[6,64,8,2,56]{4,3,2,1,0:T(2,128)S(1)} reshape(f32[6,64,8,112]{3,2,1,0:T(8,128)} %pad.20) | data formatting | bytes 2752512 | tf_op jit(solution)/shard_map/reshape | solution.py:360
  7.9 4.4 %copy.21 = f32[8,6,56,2,64]{4,3,2,1,0:T(2,128)} copy(f32[8,6,56,2,64]{2,3,0,4,1:T(2,128)S(1)} %bitcast.20) | data formatting | bytes 2752512 | tf_op jit(solution)/shard_map/transpose | solution.py:360
  12.3 2.9 %reshape.33 = f32[8,6,56,128]{3,2,1,0:T(8,128)S(1)} reshape(f32[8,6,56,2,64]{4,3,2,1,0:T(2,128)} %copy.21) | data formatting | bytes 2752512 | tf_op jit(solution)/shard_map/reshape | solution.py:361
  15.3 0.0 copy-start
  15.3 0.0 copy-start.1
  15.3 1.4 pad.21.state
  16.7 0.0 copy-done
  16.7 0.1 reshape.34
  16.8 0.1 copy.27
  16.9 0.1 broadcast_in_dim.12
  17.0 0.7 reshape.35.rho
  17.7 0.0 copy-done.1
  17.7 0.5 pad_bitcast_fusion.noise
  18.3 120.6 %admm.1 = f32[8,6,64,128]{3,2,1,0:T(8,128)} custom-call(f32[8,6,64,128]{3,2,1,0:T(8,128)} %pad.21.state, f32[64,128]{1,0:T(8,128)} %reshape.35.rho, f32[1,128]{1,0:T(1,128)} %pad_bitcast_fusion.noise, f32[2,100,8,1024]{3,2,1,0:T(8,128)} %bitcast.22, f32[2,8,1024]{2,1,0:T(8,128)} %vis.1, s32[1,1024]{1,0:T(1,128)} %bitcast.23, s32[1,1024]{1,0:T(1,128)} %bitcast.24), custom_call_target="tpu_custom_call" | custom-call | tf_op jit(solution)/shard_map/admm/pallas_call | solution.py:396
  138.9 0.0 slice-start
  138.9 1.3 slice-done
  140.2 3.1 %reshape.36 = f32[8,6,56,2,64]{4,3,2,1,0:T(2,128)} reshape(f32[8,6,56,128]{3,2,1,0:T(8,128)S(1)} %slice-done) | data formatting | bytes 2752512 | tf_op jit(solution)/shard_map/reshape | solution.py:366
  143.3 5.4 %copy.23 = f32[8,6,56,2,64]{2,3,0,4,1:T(2,128)S(1)} copy(f32[8,6,56,2,64]{4,3,2,1,0:T(2,128)} %reshape.36) | data formatting | bytes 2752512 | tf_op jit(solution)/shard_map/reshape | solution.py:366
  148.7 2.7 %reshape.37 = f32[6,64,8,112]{3,2,1,0:T(8,128)} reshape(f32[6,64,8,2,56]{4,3,2,1,0:T(2,128)S(1)} %bitcast.21) | data formatting | bytes 2752512 | tf_op jit(solution)/shard_map/reshape | solution.py:367
  151.5 1.4 fusion
  152.9 0.2 slice.27
  153.1 1.1 copy.24
  154.2 0.2 slice.29
  154.4 1.1 copy.25
  155.5 0.2 slice.31
  155.8 1.1 copy.26
  (2 shorter events, 0.0 us)
Async XLA Ops:
  15.3 1.4 copy-start
  15.3 2.4 %copy-start.1 = (f32[100]{0:T(128)S(1)}, f32[100]{0:T(128)}, u32[]{:S(2)}) copy-start(f32[100]{0:T(128)} %param.17) | copy-start | bytes 1204
  138.9 1.3 slice-start

commit v4 on v3

--- a/solution.py
+++ b/solution.py
@@ -8,7 +8,6 @@
 
 ITERS = 4
 LANES = 128
-HALF = 64
 CHUNK = 256
 TILE = 16
 
@@ -37,53 +36,24 @@
     lax.fori_loop(0, count, eliminate, 0)
 
 
-def arrange_smoother(level, work, smooth, first_band, position, half_k):
-    bands, count, piece, _ = smooth.shape
-    lanes = level.shape[1]
-    cols = lax.broadcasted_iota(jnp.int32, (count, lanes), 0)
-    mats = []
-    for f in range(bands):
-        eye = jnp.where(cols == first_band + f, 1.0, 0.0)
-        mats.append(eye - level * work[first_band + f])
-    mats = jnp.concatenate(mats, axis=0)
-    hi = mats.astype(jnp.bfloat16)
-    rest = mats - hi.astype(jnp.float32)
-    mid = rest.astype(jnp.bfloat16)
-    low = (rest - mid.astype(jnp.float32)).astype(jnp.bfloat16)
-    direction = lax.broadcasted_iota(jnp.int32, (lanes, LANES), 0)
-    lane = lax.broadcasted_iota(jnp.int32, (lanes, LANES), 1)
-    for j in range(piece):
-        wanted = jnp.where(lane < HALF, 0, half_k) + position + j
-        pick = jnp.where(direction == wanted, 1.0, 0.0).astype(jnp.bfloat16)
-        rows = sum(jnp.dot(x, pick, preferred_element_type=jnp.float32) for x in (hi, mid, low))
-        for f in range(bands):
-            smooth[f, :, j, :] = rows[f * count : (f + 1) * count]
-
-
-def build_tables(first, second, t1, t2, tt):
-    rows = t1.shape[1]
-    slot = lax.rem(lax.broadcasted_iota(jnp.int32, (LANES, CHUNK), 0), HALF)
+def build_tables(first, second, t1, t2, ts):
+    twice, rows = t1.shape
+    count = twice // 2
+    slot = lax.rem(lax.broadcasted_iota(jnp.int32, (twice, CHUNK), 0), count)
     for rc in range(rows // CHUNK):
         rsl = pl.ds(rc * CHUNK, CHUNK)
         for side, (stations, table) in enumerate(((first, t1), (second, t2))):
-            hot = jnp.where(slot == stations[:, rsl], 1.0, 0.0)
-            table[:, rsl] = hot.astype(jnp.bfloat16)
-            turned = jnp.transpose(hot).astype(jnp.bfloat16)
+            hot = jnp.where(slot == stations[:, rsl], 1.0, 0.0).astype(jnp.bfloat16)
+            table[:, rsl] = hot
             for part in range(2):
-                tt[rc, pl.ds((2 * side + part) * CHUNK, CHUNK), :] = turned
-
-
-def band_sums(g_re, g_im, load_c, load_v, rows, t1, t2, tt, gp, gq, xs):
-    half_k = g_re.shape[0]
-    full_k = 2 * half_k
-    lane = lax.broadcasted_iota(jnp.int32, (half_k, LANES), 1)
-    low = lane < HALF
+                ts[rc, :, pl.ds((2 * side + part) * CHUNK, CHUNK)] = hot[:count]
+
+
+def band_sums(g_re, g_im, load_c, load_v, rows, full_k, t1, t2, ts, gp, gq, xs):
     parts = []
     for g in (g_re, g_im):
-        r = pltpu.roll(g, HALF, 1)
-        for full in (jnp.where(low, g, r), jnp.where(low, r, g)):
-            hi = full.astype(jnp.bfloat16).astype(jnp.float32)
-            parts.append(jnp.where(low, hi, full - hi))
+        hi = g.astype(jnp.bfloat16).astype(jnp.float32)
+        parts.append(jnp.transpose(jnp.concatenate([hi, g - hi], axis=0))[:full_k])
     lhs = jnp.concatenate(parts, axis=0).astype(jnp.bfloat16)
     total = None
 
@@ -104,7 +74,7 @@
         def put(kind, kt, side, x):
             hi = x.astype(jnp.bfloat16)
             lo = (x - hi.astype(jnp.float32)).astype(jnp.bfloat16)
-            rsel = pl.ds(kind * full_k + kt * TILE, TILE)
+            rsel = pl.ds(kind * LANES + kt * TILE, TILE)
             xs[buf, rsel, pl.ds(2 * side * CHUNK, CHUNK)] = hi
             xs[buf, rsel, pl.ds((2 * side + 1) * CHUNK, CHUNK)] = lo
 
@@ -131,15 +101,11 @@
             put(1, kt, 0, d_re * q_im + d_im * q_re)
             put(0, kt, 1, d_re * p_re + d_im * p_im)
             put(1, kt, 1, d_re * p_im - d_im * p_re)
-        part = jnp.dot(xs[buf], tt[rc], preferred_element_type=jnp.float32)
+        part = lax.dot_general(ts[rc], xs[buf], (((1,), (1,)), ((), ())), preferred_element_type=jnp.float32)
         total = part if total is None else total + part
 
-    def pack(kind):
-        x = total[kind * full_k : (kind + 1) * full_k]
-        return jnp.where(low, x[:half_k], x[half_k:])
-
-    den = pack(2)
-    return pack(0) + g_re * den, pack(1) + g_im * den, den
+    num_re, num_im, den = (total[:, i * LANES : (i + 1) * LANES] for i in range(3))
+    return num_re + g_re * den, num_im + g_im * den, den
 
 
 MESH = pl.DeviceIdType.MESH
@@ -147,16 +113,17 @@
 
 
 def fused_kernel(
-    half_k, steps, weight_per_rho,
-    state, rho, noise, coh_hbm, vis, first, second,
-    out,
-    t1, t2, tt, work, smooth, coh, tail, gfull, cfull, psend, yrecv, zbuf, zrecv, mix, mixrecv, gp, gq, xs,
+    steps, weight_per_rho,
+    gains_start, consensus_prev, dual_prev, levels, coh_hbm, vis, first, second,
+    gains_out, cons_out, dual_out,
+    t1, t2, ts, work, state, coh, tail, gfull, cfull, psend, yrecv, zbuf, zrecv, mix, mixrecv, gp, gq, xs,
     coh_sem, ysend_sem, yrecv_sem, zsend_sem, zrecv_sem, gz_send, gz_recv, gy_send, gy_recv,
     mix_send, mix_recv, cz_send, cz_recv, cy_send, cy_recv,
 ):
     bands, _, packed, _ = gfull.shape
     directions = coh_hbm.shape[1]
     whole = directions // TILE * TILE
+    full_k = round_up(directions, TILE)
     rows = t1.shape[1]
     nblk, nband = lax.axis_size("blk"), lax.axis_size("band")
     nz = nblk // 2
@@ -217,10 +184,27 @@
         pl.semaphore_signal(barrier, inc=1, device_id=peer(d), device_id_type=MESH)
     for d in range(1, nband):
         pl.semaphore_signal(barrier, inc=1, device_id=band_peer(d), device_id_type=MESH)
-    gfull[...] = state[:, 0:2]
-    psend[...] = jnp.zeros_like(psend)
+    stations = gains_start.shape[1]
+    rho, noise = levels[0:1], levels[1:2]
+
+    def window(ref, c, f):
+        begin = f * directions
+        at = min(begin, bands * directions - LANES)
+        value = ref[c, :, at : at + LANES]
+        return pltpu.roll(value, LANES - (begin - at), 1) if begin > at else value
+
+    if packed > stations:
+        gfull[:, :, stations:] = jnp.zeros((bands, 2, packed - stations, LANES), jnp.float32)
+        state[:, :, stations:] = jnp.zeros((bands, 4, packed - stations, LANES), jnp.float32)
+    for f in range(bands):
+        for c in range(2):
+            gfull[f, c, :stations] = window(gains_start, c, f)
+            scaled = window(dual_prev, c, f) / rho
+            state[f, c, :stations] = window(consensus_prev, c, f) - scaled
+            state[f, 2 + c, :stations] = scaled
+    xs[...] = jnp.zeros_like(xs)
     tail[...] = jnp.zeros_like(tail)
-    build_tables(first, second, t1, t2, tt)
+    build_tables(first, second, t1, t2, ts)
     pl.semaphore_wait(barrier, nz + nband - 1)
 
     def compute(n):
@@ -247,10 +231,9 @@
         def load_v(rsl):
             return vis[0, pl.ds(f, 1), rsl], vis[1, pl.ds(f, 1), rsl]
 
-        g_re, g_im = gfull[f, 0, :half_k], gfull[f, 1, :half_k]
-        sums = band_sums(g_re, g_im, load_c, load_v, rows, t1, t2, tt, gp, gq, xs)
+        sums = band_sums(gfull[f, 0], gfull[f, 1], load_c, load_v, rows, full_k, t1, t2, ts, gp, gq, xs)
         for i in range(3):
-            psend[f, i, :half_k] = sums[i]
+            psend[f, i] = sums[i]
         y_copy(f).start()
 
     def stage_b(n):
@@ -266,14 +249,13 @@
         for d in range(1, nz):
             z_copy(f, d).wait()
             total = total + zrecv[f, d - 1]
-        w = rho[own] * weight_per_rho
+        w = rho * weight_per_rho
         inverse = 0.5 / (total[2] + w)
         for c in range(2):
-            scaled = state[f, 4 + c, own] / rho[own]
-            fresh = (total[c] + w * (state[f, 2 + c, own] - scaled)) * inverse
+            fresh = (total[c] + w * state[f, c, own]) * inverse
             value = 0.5 * gfull[f, c, own] + fresh
             gfull[f, c, own] = value
-            mix[f, c] = value + scaled
+            mix[f, c] = value + state[f, 2 + c, own]
         for d in range(1, nz):
             all_z(gfull, gz_send, gz_recv, f, d, False).start()
 
@@ -301,13 +283,12 @@
 
         @pl.when(n == steps + LAG_B - 1)
         def _():
-            invert(smooth.shape[1], noise[...], work)
+            invert(work.shape[0], noise, work)
 
         return carry
 
     lax.fori_loop(0, steps + LAG_D, turn, 0)
 
-    arrange_smoother(noise[...], work, smooth, group * bands, y * half + z * piece, half_k)
     for d in range(1, nband):
         for f in range(bands):
             mix_copy(f, d).wait()
@@ -317,7 +298,9 @@
         for d in range(nband):
             source = lax.rem(group + nband - d, nband)
             for h in range(bands):
-                w = smooth[f, source * bands + h]
+                column = source * bands + h
+                unit = jnp.where(column == group * bands + f, 1.0, 0.0)
+                w = unit - noise * work[group * bands + f, pl.ds(column, 1), :]
                 for c in range(2):
                     acc[c] += w * (mix[h, c] if d == 0 else mixrecv[d - 1, h, c])
         for c in range(2):
@@ -337,37 +320,21 @@
 
     lax.fori_loop(0, bands, spread_y, 0)
 
-    def finish(f, carry):
+    for f in range(bands):
         all_y(gfull, gy_send, gy_recv, f, False).wait_send()
         all_y(gfull, gy_send, gy_recv, f, True).wait_recv()
+        at = pl.ds(f * directions, directions)
+        for c in range(2):
+            gains_out[c, :, at] = gfull[f, c, :stations, :directions]
+    for f in range(bands):
         all_y(cfull, cy_send, cy_recv, f, False).wait_send()
         all_y(cfull, cy_send, cy_recv, f, True).wait_recv()
+        at = pl.ds(f * directions, directions)
         for c in range(2):
-            g, cons = gfull[f, c], cfull[f, c]
-            out[f, c] = g
-            out[f, 2 + c] = cons
-            out[f, 4 + c] = state[f, 4 + c] + rho[...] * (g - cons)
-        return carry
-
-    lax.fori_loop(0, bands, finish, 0)
-
-
-def packer(stations, bands, directions, half_k, packed):
-    def pack(x):
-        c = x.shape[0]
-        x = x.reshape(c, x.shape[1], bands, directions)
-        x = jnp.pad(x, ((0, 0), (0, HALF - x.shape[1]), (0, 0), (0, 2 * half_k - directions)))
-        x = x.reshape(c, HALF, bands, 2, half_k).transpose(2, 0, 4, 3, 1)
-        x = x.reshape(bands, c, half_k, LANES)
-        return jnp.pad(x, ((0, 0), (0, 0), (0, packed - half_k), (0, 0)))
-
-    def unpack(x):
-        c = x.shape[1]
-        x = x[:, :, :half_k].reshape(bands, c, half_k, 2, HALF).transpose(1, 4, 0, 3, 2)
-        x = x.reshape(c, HALF, bands, 2 * half_k)[:, :stations, :, :directions]
-        return x.reshape(c, stations, bands * directions)
-
-    return pack, unpack
+            cons = cfull[f, c, :stations]
+            change = rho * (gfull[f, c, :stations] - cons)
+            cons_out[c, :, at] = cons[:, :directions]
+            dual_out[c, :, at] = dual_prev[c, :, at] + change[:, :directions]
 
 
 def on_device(visibility, coherency, station_first, station_second, gains_start, consensus_prev, dual_prev, penalty, noise_var):
@@ -379,31 +346,24 @@
     nband = lax.axis_size("band")
     bands_all = bands * nband
     full_k = round_up(directions, TILE)
-    half_k = full_k // 2
-    packed = round_up(half_k, 8 * groups)
+    packed = round_up(stations, 8 * groups)
     piece = packed // groups
     nz = groups // 2
-    pack, unpack = packer(stations, bands, directions, half_k, packed)
-    rho = jnp.pad(penalty, (0, full_k - directions), constant_values=1.0).reshape(2, half_k).T
-    rho = jnp.pad(rho, ((0, packed - half_k), (0, 0)), constant_values=1.0)
-    rho = jnp.repeat(rho, HALF, axis=1)
-    lanes = round_up(full_k, LANES)
-    noise = jnp.pad(noise_var, (0, lanes - directions), constant_values=1.0)[None, :]
-    state = pack(jnp.concatenate([gains_start, consensus_prev, dual_prev], axis=0))
+    levels = jnp.pad(jnp.stack([penalty, noise_var]), ((0, 0), (0, LANES - directions)), constant_values=1.0)
     vmem = pl.BlockSpec(memory_space=pltpu.VMEM)
     dma = pltpu.SemaphoreType.DMA
     f32, bf16 = jnp.float32, jnp.bfloat16
     out = pl.pallas_call(
-        functools.partial(fused_kernel, half_k, ITERS * bands, rows * groups / (stations * directions)),
-        out_shape=jax.ShapeDtypeStruct((bands, 6, packed, LANES), f32),
-        in_specs=[vmem] * 3 + [pl.BlockSpec(memory_space=pl.ANY)] + [vmem] * 3,
-        out_specs=vmem,
+        functools.partial(fused_kernel, ITERS * bands, rows * groups / (stations * directions)),
+        out_shape=(jax.ShapeDtypeStruct(gains_start.shape, f32),) * 3,
+        in_specs=[vmem] * 4 + [pl.BlockSpec(memory_space=pl.ANY)] + [vmem] * 3,
+        out_specs=(vmem, vmem, vmem),
         scratch_shapes=[
-            pltpu.VMEM((LANES, rows), bf16),
-            pltpu.VMEM((LANES, rows), bf16),
-            pltpu.VMEM((rows // CHUNK, 4 * CHUNK, LANES), bf16),
-            pltpu.VMEM((bands_all, bands_all, lanes), f32),
-            pltpu.VMEM((bands, bands_all, piece, LANES), f32),
+            pltpu.VMEM((2 * packed, rows), bf16),
+            pltpu.VMEM((2 * packed, rows), bf16),
+            pltpu.VMEM((rows // CHUNK, packed, 4 * CHUNK), bf16),
+            pltpu.VMEM((bands_all, bands_all, LANES), f32),
+            pltpu.VMEM((bands, 4, packed, LANES), f32),
             pltpu.VMEM((bands, 2, directions, rows), f32),
             pltpu.VMEM((bands, 2, TILE, rows), f32),
             pltpu.VMEM((bands, 2, packed, LANES), f32),
@@ -416,7 +376,7 @@
             pltpu.VMEM((nband - 1, bands, 2, piece, LANES), f32),
             pltpu.VMEM((2, 2 * full_k, CHUNK), f32),
             pltpu.VMEM((2, 2 * full_k, CHUNK), f32),
-            pltpu.VMEM((2, 3 * full_k, 4 * CHUNK), bf16),
+            pltpu.VMEM((2, 3 * LANES, 4 * CHUNK), bf16),
             dma((bands,)),
             dma((bands,)), dma((bands,)),
             dma((bands, nz - 1)), dma((bands, nz - 1)),
@@ -428,9 +388,8 @@
         ],
         compiler_params=pltpu.CompilerParams(collective_id=0, has_side_effects=True, vmem_limit_bytes=56 << 20),
         name="admm",
-    )(state, rho, noise, coherency.transpose(0, 2, 1, 3), visibility, station_first[None, :], station_second[None, :])
-    out = unpack(out)
-    return (out[0:2], out[2:4], out[4:6])
+    )(gains_start, consensus_prev, dual_prev, levels, coherency.transpose(0, 2, 1, 3), visibility, station_first[None, :], station_second[None, :])
+    return out
 
 
 def solution(mesh):

time: 157 us -> 134 us (0.85)
  local copies, waits for them, and re-layouts: 33.6 us -> 11.8 us
    reshape x9 -> x0, local copies, waits for them, and re-layouts: 19 us -> none  [the longest x2 8.46 us: unpack(): x[:, :, :half_k].reshape(bands, c, half_k, 2, HALF).transpose(1, 4, 0, 3, 2)]
    pallas_call x0 -> x3, local copies, waits for them, and re-layouts: none -> 6.37 us  [on_device(): pl.pallas_call(functools.partial(fused_kernel, ITERS * bands, rows * grou...]
    transpose x1 -> x0, local copies, waits for them, and re-layouts: 4.45 us -> none  [pack(): x = x.reshape(c, HALF, bands, 2, half_k).transpose(2, 0, 4, 3, 1)]
    slice x6 -> x0, local copies, waits for them, and re-layouts: 3.42 us -> none  [the longest x4 2.09 us: on_device(): return (out[0:2], out[2:4], out[4:6])]
    pad x4 -> x0, local copies, waits for them, and re-layouts: 2.65 us -> none  [the longest x1 1.38 us: pack(): return jnp.pad(x, ((0, 0), (0, 0), (0, packed - half_k), (0, 0)))]
    unnamed x8 -> x3, local copies, waits for them, and re-layouts: 3.43 us -> 5.47 us
    concatenate x1 -> x0, other arithmetic: 1.87 us -> none  [on_device(): jnp.concatenate([gains_start, consensus_prev, dual_prev], axis=0)]
where the time goes in v4:
time: 134 us
  Pallas kernels  120 us (90%)
  local copies, waits for them, and re-layouts  11.8 us (9%)
    pallas_call x1, Pallas kernels, on_device(): pl.pallas_call(functools.partial(fused_kernel, ITERS * bands, rows * grou...  120 us
    pallas_call x3, local copies, waits for them, and re-layouts, on_device(): pl.pallas_call(functools.partial(fused_kernel, ITERS * bands, rows * grou...  6.37 us
    unnamed x3, local copies, waits for them, and re-layouts  5.47 us

profile of v4, /device:TPU:0, one launch (start us, length us, event | category | flops | bytes accessed | tf_op | source)
XLA Modules:
  0.0 133.8 jit_solution(2282591854011992627)
XLA Ops:
  0.6 1.2 select_maximum_fusion.levels
  1.9 1.8 %copy.12.gains_start = f32[2,62,800]{2,1,0:T(8,128)} copy(f32[2,62,800]{2,0,1:T(2,128)} %param.13) | data formatting | bytes 793600 | tf_op args[4]
  3.7 1.8 %copy.13.consensus_prev = f32[2,62,800]{2,1,0:T(8,128)} copy(f32[2,62,800]{2,0,1:T(2,128)} %param.14) | data formatting | bytes 793600 | tf_op args[5]
  5.5 1.8 %copy.14.dual_prev = f32[2,62,800]{2,1,0:T(8,128)} copy(f32[2,62,800]{2,0,1:T(2,128)} %param.15) | data formatting | bytes 793600 | tf_op args[6]
  7.3 120.1 %admm.1 = (f32[2,62,800]{2,1,0:T(8,128)}, f32[2,62,800]{2,1,0:T(8,128)}, f32[2,62,800]{2,1,0:T(8,128)}) custom-call(f32[2,62,800]{2,1,0:T(8,128)} %copy.12.gains_start, f32[2,62,800]{2,1,0:T(8,128)} %copy.13.consensus_prev, f32[2,62,800]{2,1,0:T(8,128)} %copy.14.dual_prev, f32[2,128]{1,0:T(2,128)} %select_maximum_fusion.levels, f32[2,100,8,1024]{3,2,1,0:T(8,128)} %bitcast.5, ...), custom_call_target="tpu_custom_call" | custom-call | tf_op jit(solution)/shard_map/admm/pallas_call | solution.py:356
  127.4 2.1 %copy.15 = f32[2,62,800]{2,0,1:T(2,128)} copy(f32[2,62,800]{2,1,0:T(8,128)} %get-tuple-element.3) | data formatting | bytes 793600 | tf_op jit(solution)/shard_map/admm/pallas_call | solution.py:356
  129.5 2.1 %copy.16 = f32[2,62,800]{2,0,1:T(2,128)} copy(f32[2,62,800]{2,1,0:T(8,128)} %get-tuple-element.4) | data formatting | bytes 793600 | tf_op jit(solution)/shard_map/admm/pallas_call | solution.py:356
  131.7 2.1 %copy.17 = f32[2,62,800]{2,0,1:T(2,128)} copy(f32[2,62,800]{2,1,0:T(8,128)} %get-tuple-element.5) | data formatting | bytes 793600 | tf_op jit(solution)/shard_map/admm/pallas_call | solution.py:356

commit v5 on v4

--- a/solution.py
+++ b/solution.py
@@ -114,8 +114,9 @@
 
 def fused_kernel(
     steps, weight_per_rho,
-    gains_start, consensus_prev, dual_prev, levels, coh_hbm, vis, first, second,
-    gains_out, cons_out, dual_out,
+    gains_hbm, cons_hbm, dual_hbm, levels, coh_hbm, vis, first, second,
+    gains_to, cons_to, dual_to,
+    gains_start, consensus_prev, dual_prev, gains_out, cons_out, dual_out, in_sem, out_sem,
     t1, t2, ts, work, state, coh, tail, gfull, cfull, psend, yrecv, zbuf, zrecv, mix, mixrecv, gp, gq, xs,
     coh_sem, ysend_sem, yrecv_sem, zsend_sem, zrecv_sem, gz_send, gz_recv, gy_send, gy_recv,
     mix_send, mix_recv, cz_send, cz_recv, cy_send, cy_recv,
@@ -176,6 +177,17 @@
     def mix_copy(f, d):
         return remote(mix.at[f], mixrecv.at[d - 1, f], mix_send.at[f, d - 1], mix_recv.at[f, d - 1], band_peer(d))
 
+    def load_copy(i, c):
+        pair = ((gains_hbm, gains_start), (cons_hbm, consensus_prev), (dual_hbm, dual_prev))[i]
+        return pltpu.make_async_copy(pair[0].at[:, c], pair[1].at[c], in_sem.at[i, c])
+
+    def store_copy(i, c):
+        pair = ((gains_out, gains_to), (cons_out, cons_to), (dual_out, dual_to))[i]
+        return pltpu.make_async_copy(pair[0].at[c], pair[1].at[:, c], out_sem.at[i, c])
+
+    halves = [(i, c) for i in range(3) for c in range(2)]
+    for i, c in halves:
+        load_copy(i, c).start()
     for f in range(bands):
         coh_copy(f).start()
     barrier = pltpu.get_barrier_semaphore()
@@ -193,6 +205,11 @@
         value = ref[c, :, at : at + LANES]
         return pltpu.roll(value, LANES - (begin - at), 1) if begin > at else value
 
+    build_tables(first, second, t1, t2, ts)
+    xs[...] = jnp.zeros_like(xs)
+    tail[...] = jnp.zeros_like(tail)
+    for i, c in halves:
+        load_copy(i, c).wait()
     if packed > stations:
         gfull[:, :, stations:] = jnp.zeros((bands, 2, packed - stations, LANES), jnp.float32)
         state[:, :, stations:] = jnp.zeros((bands, 4, packed - stations, LANES), jnp.float32)
@@ -202,9 +219,6 @@
             scaled = window(dual_prev, c, f) / rho
             state[f, c, :stations] = window(consensus_prev, c, f) - scaled
             state[f, 2 + c, :stations] = scaled
-    xs[...] = jnp.zeros_like(xs)
-    tail[...] = jnp.zeros_like(tail)
-    build_tables(first, second, t1, t2, ts)
     pl.semaphore_wait(barrier, nz + nband - 1)
 
     def compute(n):
@@ -326,6 +340,8 @@
         at = pl.ds(f * directions, directions)
         for c in range(2):
             gains_out[c, :, at] = gfull[f, c, :stations, :directions]
+    for c in range(2):
+        store_copy(0, c).start()
     for f in range(bands):
         all_y(cfull, cy_send, cy_recv, f, False).wait_send()
         all_y(cfull, cy_send, cy_recv, f, True).wait_recv()
@@ -335,6 +351,11 @@
             change = rho * (gfull[f, c, :stations] - cons)
             cons_out[c, :, at] = cons[:, :directions]
             dual_out[c, :, at] = dual_prev[c, :, at] + change[:, :directions]
+    for c in range(2):
+        store_copy(1, c).start()
+        store_copy(2, c).start()
+    for i, c in halves:
+        store_copy(i, c).wait()
 
 
 def on_device(visibility, coherency, station_first, station_second, gains_start, consensus_prev, dual_prev, penalty, noise_var):
@@ -351,14 +372,17 @@
     nz = groups // 2
     levels = jnp.pad(jnp.stack([penalty, noise_var]), ((0, 0), (0, LANES - directions)), constant_values=1.0)
     vmem = pl.BlockSpec(memory_space=pltpu.VMEM)
+    anywhere = pl.BlockSpec(memory_space=pl.ANY)
     dma = pltpu.SemaphoreType.DMA
     f32, bf16 = jnp.float32, jnp.bfloat16
     out = pl.pallas_call(
         functools.partial(fused_kernel, ITERS * bands, rows * groups / (stations * directions)),
-        out_shape=(jax.ShapeDtypeStruct(gains_start.shape, f32),) * 3,
-        in_specs=[vmem] * 4 + [pl.BlockSpec(memory_space=pl.ANY)] + [vmem] * 3,
-        out_specs=(vmem, vmem, vmem),
+        out_shape=(jax.ShapeDtypeStruct((stations, 2, bands * directions), f32),) * 3,
+        in_specs=[anywhere] * 3 + [vmem, anywhere] + [vmem] * 3,
+        out_specs=(anywhere,) * 3,
         scratch_shapes=[
+            *[pltpu.VMEM((2, stations, bands * directions), f32)] * 6,
+            dma((3, 2)), dma((3, 2)),
             pltpu.VMEM((2 * packed, rows), bf16),
             pltpu.VMEM((2 * packed, rows), bf16),
             pltpu.VMEM((rows // CHUNK, packed, 4 * CHUNK), bf16),
@@ -388,8 +412,8 @@
         ],
         compiler_params=pltpu.CompilerParams(collective_id=0, has_side_effects=True, vmem_limit_bytes=56 << 20),
         name="admm",
-    )(gains_start, consensus_prev, dual_prev, levels, coherency.transpose(0, 2, 1, 3), visibility, station_first[None, :], station_second[None, :])
-    return out
+    )(*(x.transpose(1, 0, 2) for x in (gains_start, consensus_prev, dual_prev)), levels, coherency.transpose(0, 2, 1, 3), visibility, station_first[None, :], station_second[None, :])
+    return tuple(x.transpose(1, 0, 2) for x in out)
 
 
 def solution(mesh):

time: 134 us -> 129 us (0.963)
  local copies, waits for them, and re-layouts: 11.8 us -> 5.51 us
    pallas_call x3 -> x0, local copies, waits for them, and re-layouts: 6.37 us -> none  [on_device(): pl.pallas_call(functools.partial(fused_kernel, ITERS * bands, rows * grou...]
where the time goes in v5:
time: 129 us; the launch traced here: 128 us
  Pallas kernels  121 us (94%)
  local copies, waits for them, and re-layouts  5.51 us (4%)
    pallas_call x1, Pallas kernels, on_device(): pl.pallas_call(functools.partial(fused_kernel, ITERS * bands, rows * grou...  121 us
    unnamed x3, local copies, waits for them, and re-layouts  5.51 us

profile of v5, /device:TPU:0, one launch (start us, length us, event | category | flops | bytes accessed | tf_op | source)
XLA Modules:
  0.0 128.3 jit_solution(11997545176596829853)
XLA Ops:
  0.6 1.2 select_maximum_fusion.levels
  1.9 121.0 %admm.1 = (f32[62,2,800]{2,1,0:T(2,128)}, f32[62,2,800]{2,1,0:T(2,128)}, f32[62,2,800]{2,1,0:T(2,128)}) custom-call(f32[62,2,800]{2,1,0:T(2,128)} %bitcast.12, f32[62,2,800]{2,1,0:T(2,128)} %bitcast.13, f32[62,2,800]{2,1,0:T(2,128)} %bitcast.14, f32[2,128]{1,0:T(2,128)} %select_maximum_fusion.levels, f32[2,100,8,1024]{3,2,1,0:T(8,128)} %bitcast.11, ...), custom_call_target="tpu_custom_call" | custom-call | tf_op jit(solution)/shard_map/admm/pallas_call | solution.py:378
  122.8 1.8 %copy.15 = f32[2,62,800]{2,0,1:T(2,128)} copy(f32[2,62,800]{2,0,1:T(2,128)} %bitcast.17) | data formatting | bytes 793600
  124.7 1.8 %copy.16 = f32[2,62,800]{2,0,1:T(2,128)} copy(f32[2,62,800]{2,0,1:T(2,128)} %bitcast.16) | data formatting | bytes 793600
  126.5 1.8 %copy.17 = f32[2,62,800]{2,0,1:T(2,128)} copy(f32[2,62,800]{2,0,1:T(2,128)} %bitcast.15) | data formatting | bytes 793600

commit v6 on v5

--- a/solution.py
+++ b/solution.py
@@ -109,7 +109,7 @@
 
 
 MESH = pl.DeviceIdType.MESH
-LAG_B, LAG_C, LAG_D = 2, 4, 6
+LAG_B, LAG_C, LAG_D = 1, 3, 5
 
 
 def fused_kernel(

time: 129 us -> 127 us (0.984)
  Pallas kernels: 121 us -> 119 us
    pallas_call x1, Pallas kernels: 121 us -> 119 us  [on_device(): pl.pallas_call(functools.partial(fused_kernel, ITERS * bands, rows * grou...]
where the time goes in v6:
time: 127 us
  Pallas kernels  119 us (94%)
  local copies, waits for them, and re-layouts  5.51 us (4%)
    pallas_call x1, Pallas kernels, on_device(): pl.pallas_call(functools.partial(fused_kernel, ITERS * bands, rows * grou...  119 us
    unnamed x3, local copies, waits for them, and re-layouts  5.51 us

profile of v6, /device:TPU:0, one launch (start us, length us, event | category | flops | bytes accessed | tf_op | source)
XLA Modules:
  0.0 126.5 jit_solution(3831493116231216158)
XLA Ops:
  0.6 1.2 select_maximum_fusion.levels
  1.9 119.1 %admm.1 = (f32[62,2,800]{2,1,0:T(2,128)}, f32[62,2,800]{2,1,0:T(2,128)}, f32[62,2,800]{2,1,0:T(2,128)}) custom-call(f32[62,2,800]{2,1,0:T(2,128)} %bitcast.12, f32[62,2,800]{2,1,0:T(2,128)} %bitcast.13, f32[62,2,800]{2,1,0:T(2,128)} %bitcast.14, f32[2,128]{1,0:T(2,128)} %select_maximum_fusion.levels, f32[2,100,8,1024]{3,2,1,0:T(8,128)} %bitcast.11, ...), custom_call_target="tpu_custom_call" | custom-call | tf_op jit(solution)/shard_map/admm/pallas_call | solution.py:378
  121.0 1.8 %copy.15 = f32[2,62,800]{2,0,1:T(2,128)} copy(f32[2,62,800]{2,0,1:T(2,128)} %bitcast.17) | data formatting | bytes 793600
  122.8 1.8 %copy.16 = f32[2,62,800]{2,0,1:T(2,128)} copy(f32[2,62,800]{2,0,1:T(2,128)} %bitcast.16) | data formatting | bytes 793600
  124.7 1.8 %copy.17 = f32[2,62,800]{2,0,1:T(2,128)} copy(f32[2,62,800]{2,0,1:T(2,128)} %bitcast.15) | data formatting | bytes 793600
